TPU v7x, 32 devices: a whole 2x2x4 slice. The times are simulated.
32 devices in a mesh: grp: 4 (over x, core), dev: 8 (over z, y).
Axes of the slice: x: 2, y: 2, z: 4, core: 2. Of those that a mesh axis runs over, the one named last changes fastest.
Arguments:
- residual: bfloat16 [4096, 2048], P(('grp', 'dev')), may hold values from -3 to 3
- queries: bfloat16 [4096, 1024], P(('grp', 'dev')), may hold values from -9 to 9
- keys: bfloat16 [4096, 256], P(('grp', 'dev')), may hold values from -6 to 6
- values: bfloat16 [4096, 256], P(('grp', 'dev')), may hold values from -18 to 18
- prefix_keys: bfloat16 [16, 512, 256], P('grp', 'dev'), may hold values from -6 to 6
- cached_prefix_values: bfloat16 [16, 512, 256], P('grp', 'dev'), may hold values from -18 to 18
- out_weight: bfloat16 [1024, 2048], replicated, may hold values from -0.1875 to 0.1875
- norm_gain: float32 [2048], replicated, may hold values from 0.25 to 1.75
- w_gate: bfloat16 [2048, 8192], P('grp', 'dev'), may hold values from -0.125 to 0.125
- w_up: bfloat16 [2048, 8192], P('grp', 'dev'), may hold values from -0.125 to 0.125
- w_down: bfloat16 [8192, 2048], P('dev', 'grp'), may hold values from -0.0625 to 0.0625
- suffix_lengths: int32 [4, 32], P('grp'), may hold values from 1 to 128, 1024 in all within a row
- request_group: int32 [4, 32], P('grp'), may hold values from 0 to 3, as said below
- placement_order: int32 [4, 32], P('grp'), may hold values from 0 to 31, each once within a row
Outputs:
- layer_out: bfloat16 [4096, 2048], P(('grp', 'dev'))
Inputs may be any that keep to these rules, and one draw needn't show every extreme that they name: `suffix_lengths`: the 32 lengths of one row sum to 1024. `request_group`: each row names each of its 4 groups exactly 8 times. `placement_order`: each row is an ordering of its 32 requests.
All inputs are finite; a program needn't handle non-finite values.
Results may differ from a plain program's by a relative error of at most 0.012.
Values may be sent and summed in bfloat16 or wider, within the bound.
No kernel may reach another device: no remote copies, remote signals or barrier semaphores. Data moves between devices by JAX's collectives and lax.ppermute only.
A program may use at most 128 MiB of HBM per device.

v0:
```python
import functools
import math

import jax
import jax.numpy as jnp
from jax import lax
from jax.experimental import pallas as pl
from jax.experimental.pallas import tpu as pltpu
from jax.sharding import PartitionSpec as P

HEAD_SIZE = 64
NEG_FILL = -1e30
EPSILON = 1e-05
F32 = jnp.float32
BF16 = jnp.bfloat16
LANES = 2 * HEAD_SIZE
CORES = 2
HALVES = 2


def cost(microseconds):
    return pl.CostEstimate(flops=0, bytes_accessed=int(microseconds * 3.5e6), transcendentals=0)


def dot(a, b, contract_b=0):
    return lax.dot_general(
        a, b, (((1,), (contract_b,)), ((), ())), preferred_element_type=F32
    )


def prepare_body(
    span,
    lengths_hbm,
    groups_hbm,
    packing_hbm,
    queries_hbm,
    *refs,
):
    q_ref, before_ref, within_ref, prefix_ref = refs[:4]
    lengths_ref, groups_ref, packing_ref, queries_ref, sems = refs[4:]
    copies = [
        pltpu.make_async_copy(source, target, sems.at[i])
        for i, (source, target) in enumerate(
            [
                (lengths_hbm, lengths_ref),
                (groups_hbm, groups_ref),
                (packing_hbm, packing_ref),
                (queries_hbm, queries_ref),
            ]
        )
    ]
    for copy in copies:
        copy.start()
    for copy in copies:
        copy.wait()
    tokens = queries_ref.shape[0]
    pairs, rows = q_ref.shape[0], q_ref.shape[1]
    per = rows // (2 * tokens)
    base = lax.axis_index("dev") * tokens
    own = base + lax.broadcasted_iota(jnp.int32, (tokens, LANES), 0)

    def request(k, carry):
        start, group, first = carry
        j = packing_ref[0, k]
        end = start + lengths_ref[0, j]
        inside = (own >= start) & (own < end)
        return (
            end,
            jnp.where(inside, groups_ref[0, j], group),
            jnp.where(inside, start, first),
        )

    zero = jnp.zeros((tokens, LANES), jnp.int32)
    _, group, first = lax.fori_loop(0, lengths_ref.shape[1], request, (jnp.int32(0), zero, zero))
    for ref, back in ((before_ref, tokens), (within_ref, 0)):
        for c in range(0, tokens, LANES):
            key = base - back + c + lax.broadcasted_iota(jnp.int32, (tokens, LANES), 1)
            ref[:, c : c + LANES] = jnp.where((key >= first) & (key <= own), 0.0, NEG_FILL)
    for c in range(0, prefix_ref.shape[1], LANES):
        key_group = lax.div(c + lax.broadcasted_iota(jnp.int32, (tokens, LANES), 1), span)
        prefix_ref[:, c : c + LANES] = jnp.where(group == key_group, 0.0, NEG_FILL)
    low = lax.broadcasted_iota(jnp.int32, (tokens, LANES), 1) < HEAD_SIZE
    for j in range(pairs):
        for parity in range(2):
            for r in range(per):
                head = (2 * j + parity) * per + r
                block = head // 2
                q = queries_ref[:, block * LANES : (block + 1) * LANES].astype(F32) * HEAD_SIZE ** (-0.5)
                if head % 2 != parity:
                    q = pltpu.roll(q, HEAD_SIZE, 1)
                q = jnp.where(low == (parity == 0), q, 0.0)
                row = (parity * per + r) * tokens
                q_ref[j, row : row + tokens, :] = q.astype(BF16)


def prepare(groups, span, lengths, request_group, packing, queries, width):
    tokens = queries.shape[0]
    per = queries.shape[1] // width
    vmem = pl.BlockSpec(memory_space=pltpu.VMEM)
    return pl.pallas_call(
        functools.partial(prepare_body, span),
        out_shape=[
            jax.ShapeDtypeStruct((width // LANES, 2 * per * tokens, LANES), BF16),
            jax.ShapeDtypeStruct((tokens, tokens), F32),
            jax.ShapeDtypeStruct((tokens, tokens), F32),
            jax.ShapeDtypeStruct((tokens, groups * span), F32),
        ],
        in_specs=[pl.BlockSpec(memory_space=pltpu.HBM)] * 4,
        out_specs=[vmem] * 4,
        compiler_params=pltpu.CompilerParams(vmem_limit_bytes=8 * 2**20),
        scratch_shapes=[pltpu.SMEM(lengths.shape, jnp.int32)] * 3
        + [pltpu.VMEM(queries.shape, BF16), pltpu.SemaphoreType.DMA((4,))],
        cost_estimate=cost(3),
        name="prepare",
    )(lengths, request_group, packing, queries)


def attend_body(first, pieces, refs):
    q_ref, refs = refs[0], refs[1:]
    if not first:
        old_max, old_sum, old_acc = refs[:3]
        refs = refs[3:]
    kv = refs[: 3 * pieces]
    new_max, new_sum, new_acc = refs[-3:]
    pairs, rows = q_ref.shape[0], q_ref.shape[1]
    half = rows // 2
    low = lax.broadcasted_iota(jnp.int32, (half, LANES), 1) < HEAD_SIZE

    def pick(even, odd):
        return jnp.where(low, even, odd)

    for j in range(pairs):
        q = q_ref[j]
        lanes = slice(j * LANES, (j + 1) * LANES)
        scores = []
        for i in range(pieces):
            k_ref, bias_ref = kv[3 * i], kv[3 * i + 2]
            s = dot(q, k_ref[:, lanes], 1)
            keys = s.shape[1]
            bias = bias_ref[...]
            s = s.reshape(rows // bias.shape[0], bias.shape[0], keys) + bias[None]
            scores.append(s.reshape(rows, keys))
        top = functools.reduce(
            jnp.maximum, [jnp.max(s, axis=1, keepdims=True) for s in scores]
        )
        if first:
            row_max = top
            pair_max = pick(row_max[:half], row_max[half:])
        else:
            old = old_max[j]
            pair_max = jnp.maximum(old, pick(top[:half], top[half:]))
            row_max = jnp.concatenate(
                [pair_max[:, :1], pair_max[:, HEAD_SIZE : HEAD_SIZE + 1]], axis=0
            )
        total = None
        for i in range(pieces):
            v_ref = kv[3 * i + 1]
            w = jnp.exp(scores[i] - row_max).astype(BF16)
            v = v_ref[:, lanes]
            v = jnp.concatenate([v, jnp.ones_like(v)], axis=1)
            part = dot(w, v)
            total = part if total is None else total + part
        acc = pick(total[:half, :LANES], total[half:, :LANES])
        summed = pick(total[:half, LANES:], total[half:, LANES:])
        if not first:
            scale = jnp.exp(old - pair_max)
            acc = acc + scale * old_acc[j]
            summed = summed + scale * old_sum[j]
        new_max[j] = pair_max
        new_sum[j] = summed
        new_acc[j] = acc


def block_refs(refs, count):
    return [r for i in range(count) for r in (refs[2 * i].at[0], refs[2 * i].at[1], refs[2 * i + 1])]


def attend(q, state, blocks):
    pairs, rows, lanes = q.shape
    first = state is None

    def kernel(*refs):
        lead = 1 + (0 if first else 3)
        attend_body(first, len(blocks), [*refs[:lead], *block_refs(refs[lead:], len(blocks)), *refs[-3:]])

    shape = jax.ShapeDtypeStruct((pairs, rows // 2, lanes), F32)
    operands = [q] + ([] if first else list(state)) + [a for block in blocks for a in block]
    vmem = pl.BlockSpec(memory_space=pltpu.VMEM)
    return pl.pallas_call(
        kernel,
        out_shape=[shape] * 3,
        in_specs=[vmem] * len(operands),
        out_specs=[vmem] * 3,
        compiler_params=pltpu.CompilerParams(vmem_limit_bytes=20 * 2**20),
        cost_estimate=cost(1.1 * len(blocks)),
        name="attend",
    )(*operands)


def block_owner(blocks, step):
    chips = blocks // CORES
    me = lax.axis_index("grp")
    x, core = lax.div(me, CORES), lax.rem(me, CORES)
    x = lax.rem(x + chips - step // CORES, chips)
    return x * CORES + lax.rem(core + step % CORES, CORES)


def project_body(
    blocks, sum_ref, acc_ref, weight_ref, residual_ref, gain_ref, hidden_ref, normed_refs, held
):
    pairs, rows, lanes = acc_ref.shape
    tokens = residual_ref.shape[0]
    per = rows // tokens
    hidden = residual_ref[...].astype(F32)
    for j in range(pairs):
        out = (acc_ref[j] / sum_ref[j]).astype(BF16)
        for r in range(0, per, 2):
            left = jnp.concatenate(
                [out[r * tokens : (r + 1) * tokens], out[(r + 1) * tokens : (r + 2) * tokens]], axis=1
            )
            heads = [(2 * j) * per + r, (2 * j + 1) * per + r, (2 * j) * per + r + 1, (2 * j + 1) * per + r + 1]
            right = jnp.concatenate(
                [weight_ref[h * HEAD_SIZE : (h + 1) * HEAD_SIZE, :] for h in heads], axis=0
            )
            hidden = hidden + dot(left, right)
    hidden_ref[...] = hidden
    mean = jnp.mean(hidden * hidden, axis=1, keepdims=True)
    held[...] = hidden * lax.rsqrt(mean + EPSILON) * gain_ref[...]
    width = hidden.shape[1] // blocks
    for b in range(blocks):
        start = pl.multiple_of(block_owner(blocks, b) * width, width)
        half, place = divmod(b, blocks // HALVES)
        normed_refs[half][:, place * width : (place + 1) * width] = held[:, pl.ds(start, width)].astype(BF16)


def attend_project(q, state, blocks, columns, out_weight, residual, gain):
    pairs, rows, lanes = q.shape
    tokens, width = residual.shape
    count = len(blocks)

    def kernel(*refs):
        mine, (weight_ref, residual_ref, gain_ref) = refs[: 4 + 2 * count], refs[4 + 2 * count : 7 + 2 * count]
        hidden_ref, *normed_refs = refs[7 + 2 * count : 8 + 2 * count + HALVES]
        held, top, total, acc = refs[-4:]
        attend_body(False, count, [*mine[:4], *block_refs(mine[4:], count), top, total, acc])
        project_body(
            columns, total, acc, weight_ref, residual_ref, gain_ref, hidden_ref, normed_refs, held
        )

    operands = [q, *state] + [a for block in blocks for a in block]
    vmem = pl.BlockSpec(memory_space=pltpu.VMEM)
    return pl.pallas_call(
        kernel,
        out_shape=[
            jax.ShapeDtypeStruct((tokens, width), F32),
        ]
        + [jax.ShapeDtypeStruct((tokens, width // HALVES), BF16)] * HALVES,
        in_specs=[vmem] * (len(operands) + 3),
        out_specs=[vmem] * (1 + HALVES),
        scratch_shapes=[pltpu.VMEM((tokens, width), F32)]
        + [pltpu.VMEM((pairs, rows // 2, lanes), F32)] * 3,
        compiler_params=pltpu.CompilerParams(vmem_limit_bytes=20 * 2**20),
        cost_estimate=cost(1.1 * count + 2),
        name="attend_project",
    )(*operands, out_weight, residual, gain)


def rise_body(parts, blocks, refs):
    pieces = parts * HALVES
    n_refs, gates, ups = refs[:pieces], refs[pieces : pieces + blocks], refs[pieces + blocks : pieces + 2 * blocks]
    act_ref, x_ref = refs[-2:]
    tokens, width = n_refs[0].shape
    for i in range(parts):
        for half in range(HALVES):
            x_ref[i * tokens : (i + 1) * tokens, half * width : (half + 1) * width] = n_refs[i * HALVES + half][...]
    depth, hidden = gates[0].shape
    tile = math.gcd(hidden, 256)

    @pl.loop(0, hidden // tile)
    def _(t):
        cols = pl.ds(pl.multiple_of(t * tile, tile), tile)
        gate = up = None
        for b in range(blocks):
            x = x_ref[:, b * depth : (b + 1) * depth]
            g, u = dot(x, gates[b][:, cols]), dot(x, ups[b][:, cols])
            gate, up = (g, u) if gate is None else (gate + g, up + u)
        act_ref[:, cols] = (gate / (1.0 + jnp.exp(-gate)) * up).astype(BF16)


def rise(normed, gates, ups):
    parts, blocks = len(normed), len(gates)
    tokens, width = normed[0][0].shape
    hidden = gates[0].shape[1]

    def kernel(*refs):
        rise_body(parts, blocks, refs)

    vmem = pl.BlockSpec(memory_space=pltpu.VMEM)
    return pl.pallas_call(
        kernel,
        out_shape=jax.ShapeDtypeStruct((parts * tokens, hidden), BF16),
        in_specs=[vmem] * (parts * HALVES + 2 * blocks),
        out_specs=vmem,
        scratch_shapes=[pltpu.VMEM((parts * tokens, HALVES * width), BF16)],
        compiler_params=pltpu.CompilerParams(vmem_limit_bytes=12 * 2**20),
        cost_estimate=cost(1.5 * parts),
        name="rise",
    )(*[half for chunk in normed for half in chunk], *gates, *ups)


def fall_body(parts, blocks, refs):
    act_ref, downs, outs = refs[0], refs[1 : 1 + blocks], refs[1 + blocks :]
    tokens, width = outs[0].shape[0], downs[0].shape[1]
    tile = math.gcd(width, 256)
    for b in range(blocks):

        @pl.loop(0, width // tile)
        def _(t):
            term = dot(act_ref[...], downs[b][:, pl.ds(pl.multiple_of(t * tile, tile), tile)])
            cols = pl.ds(pl.multiple_of(b * width + t * tile, tile), tile)
            for i in range(parts):
                outs[i][:, cols] = term[i * tokens : (i + 1) * tokens].astype(BF16)


def fall(act, parts, downs):
    blocks = len(downs)
    shape = jax.ShapeDtypeStruct((act.shape[0] // parts, blocks * downs[0].shape[1]), BF16)

    def kernel(*refs):
        fall_body(parts, blocks, refs)

    vmem = pl.BlockSpec(memory_space=pltpu.VMEM)
    return pl.pallas_call(
        kernel,
        out_shape=[shape] * parts,
        in_specs=[vmem] * (1 + blocks),
        out_specs=[vmem] * parts,
        compiler_params=pltpu.CompilerParams(vmem_limit_bytes=12 * 2**20),
        cost_estimate=cost(0.6 * parts),
        name="fall",
    )(act, *downs)


def finish_body(blocks, hidden_ref, *refs):
    terms, out_ref = refs[:-1], refs[-1]
    each = len(terms) // HALVES
    width = out_ref.shape[1] // blocks
    for b in range(blocks):
        half, column = divmod(b, blocks // HALVES)
        place = pl.ds(pl.multiple_of(block_owner(blocks, b) * width, width), width)
        total = hidden_ref[:, place]
        for term in terms[half * each : (half + 1) * each]:
            total = total + term[:, column * width : (column + 1) * width].astype(F32)
        out_ref[:, place] = total.astype(BF16)


def finish(blocks, hidden_state, terms):
    vmem = pl.BlockSpec(memory_space=pltpu.VMEM)
    operands = [hidden_state] + [term for half in terms for term in half]
    return pl.pallas_call(
        functools.partial(finish_body, blocks),
        out_shape=jax.ShapeDtypeStruct(hidden_state.shape, BF16),
        in_specs=[vmem] * len(operands),
        out_specs=vmem,
        compiler_params=pltpu.CompilerParams(vmem_limit_bytes=8 * 2**20),
        cost_estimate=cost(1),
        name="finish",
    )(*operands)


def tie(array, *others):
    return lax.optimization_barrier((array, *others))[0] if others else array


def shards(
    grps,
    devs,
    residual,
    queries,
    keys,
    values,
    prefix_keys,
    cached_prefix_values,
    out_weight,
    norm_gain,
    w_gate,
    w_up,
    w_down,
    suffix_lengths,
    request_group,
    placement_order,
):
    depth_z = math.gcd(devs, 4)
    depth_y = devs // depth_z
    cores = CORES
    depth_x = grps // cores
    ring = list(range(0, depth_z, 2)) + list(range(1, depth_z, 2))[::-1]

    def shift(by_z, by_y):
        return [
            (
                ring[i] * depth_y + y,
                ring[(i + by_z) % depth_z] * depth_y + (y + by_y) % depth_y,
            )
            for i in range(depth_z)
            for y in range(depth_y)
        ]

    x_shift = [
        (x * cores + c, (x + 1) % depth_x * cores + c) for x in range(depth_x) for c in range(cores)
    ]
    core_swap = [(x * cores + c, x * cores + 1 - c) for x in range(depth_x) for c in range(cores)]

    def round_z(block, *others):
        return lax.ppermute(tie(block, *others), "dev", shift(1, 0))

    def along_y(block, *others):
        return [lax.ppermute(tie(block, *others), "dev", shift(0, ys)) for ys in range(1, depth_y)]

    def along_x(weight, *others):
        blocks = [weight]
        for _ in range(1, depth_x):
            blocks.append(lax.ppermute(tie(blocks[-1], *others), "grp", x_shift))
        return blocks

    def other_core(block, *others):
        return lax.ppermute(tie(block, *others), "grp", core_swap)

    tokens = queries.shape[0]
    width = keys.shape[1]
    groups, span = prefix_keys.shape[:2]

    prefix = jnp.stack([prefix_keys.reshape(-1, width), cached_prefix_values.reshape(-1, width)])
    other = along_y(prefix)
    arriving = round_z(prefix)
    own = jnp.stack([keys, values])
    before = lax.ppermute(own, "dev", [(i, i + 1) for i in range(devs - 1)])
    gate_rows = along_x(w_gate)
    q, before_mask, within_mask, prefix_mask = prepare(
        groups,
        span,
        suffix_lengths,
        request_group,
        placement_order,
        queries,
        width,
    )
    blocks = [(before, before_mask), (own, within_mask), (prefix, prefix_mask)]
    ready, state = [q, before], None
    for zs in range(1, depth_z):
        if zs == depth_z - 1:
            ready += [gate_swap, *gate_rows[1:]]
        here = tie(arriving, *other, *ready)
        if zs < depth_z - 1:
            arriving = round_z(here)
        blocks += [(b, prefix_mask) for b in other + [here]]
        other = along_y(here)
        state = attend(q, state, blocks)
        blocks, ready = [], [state[0]]
        if zs == 1:
            gate_swap = other_core(w_gate, here)
        elif zs == 2:
            up_swap = other_core(w_up, here)
    down_swap = other_core(w_down, here)
    up_rows = along_x(w_up, *gate_rows[1:], here)
    gates = [w_gate, gate_swap]
    for gate in gate_rows[1:]:
        gates += [gate, other_core(gate, here)]
    hidden_state, *normed = attend_project(
        q,
        state,
        [(b, prefix_mask) for b in other],
        grps,
        out_weight,
        tie(residual, up_swap, down_swap, *gates[2:]),
        norm_gain[None],
    )

    arrived, across = [normed], [[along_y(half) for half in normed]]
    ups, downs, acts = [w_up, up_swap], [w_down, down_swap], {}
    for zs in range(1, depth_z):
        waits = across[zs - 2] if zs > 1 else [[] for _ in normed]
        arrived.append([round_z(half, *wait) for half, wait in zip(arrived[-1], waits)])
        if zs == 1:
            for up in up_rows[1:]:
                ups += [up, other_core(up, *arrived[1], *[b for c in across[0] for b in c])]
            down_cols = along_x(w_down, *ups[3:])
        late = arrived[zs - 1][1:] if zs > 1 else []
        if zs == depth_z - 1:
            acts[1] = rise([arrived[1]] + [list(c) for c in zip(*across[1])], gates, ups)
            late = [*late, acts[1]]
        across.append([along_y(half, *late) for half in arrived[zs]])
    chunks = [[a] + [list(c) for c in zip(*b)] for a, b in zip(arrived, across)]
    for down in down_cols[1:]:
        downs += [down, other_core(down, *arrived[-1], *[b for c in across[-2] for b in c])]
    chunks[2][0] = [tie(half, *[b for c in across[-1] for b in c]) for half in chunks[2][0]]

    running, terms = [None] * HALVES, [None] * HALVES
    each = len(downs) // HALVES
    for zs in list(range(1, depth_z)) + [0]:
        act = acts[zs] if zs in acts else rise(chunks[zs], gates, ups)
        for half in range(HALVES):
            parts = fall(act, depth_y, downs[half * each : (half + 1) * each])
            if zs == 0:
                parts = [parts[0]] + [tie(part, running[half]) for part in parts[1:]]
            terms[half] = [parts[0]] + [
                lax.ppermute(parts[ys], "dev", shift(0, -ys)) for ys in range(1, depth_y)
            ]
            if running[half] is not None:
                terms[half].append(round_z(running[half]))
            if zs:
                running[half] = functools.reduce(
                    jnp.add, [term.astype(F32) for term in terms[half]]
                ).astype(BF16)
    return finish(grps, hidden_state, terms)


def solution(mesh):
    placed = (
        P(("grp", "dev"), None),
        P(("grp", "dev"), None),
        P(("grp", "dev"), None),
        P(("grp", "dev"), None),
        P("grp", "dev", None),
        P("grp", "dev", None),
        P(),
        P(),
        P("grp", "dev"),
        P("grp", "dev"),
        P("dev", "grp"),
        P("grp", None),
        P("grp", None),
        P("grp", None),
    )
    return jax.shard_map(
        functools.partial(shards, mesh.shape["grp"], mesh.shape["dev"]),
        mesh=mesh,
        in_specs=placed,
        out_specs=P(("grp", "dev"), None),
        check_vma=False,
    )
```

profile of v0, /device:TPU:0, one launch (start us, length us, event | category | flops | bytes accessed | tf_op | source)
XLA Modules:
  0.0 154.6 jit_solution(1051397150542973855)
XLA Ops:
  1.1 4.1 %collective-permute-start.2 = (bf16[2,256,256]{2,1,0:T(8,128)(2,1)S(1)}, bf16[2,256,256]{2,1,0:T(8,128)(2,1)S(1)}, u32[]{:S(2)}, u32[]{:S(2)}) collective-permute-start(bf16[2,256,256]{2,1,0:T(8,128)(2,1)S(1)} %pad_maximum_fusion.refs_5_), channel_id=1, source_target_pairs={{0,4},{1,5},{4,6},{5,7},{6,2},{7,3},{2,0},{3,1},{8,12},{9,13},{12,... | collective-permute-start | bytes 786440 | tf_op jit(solution)/shard_map/ppermute | solution.py:415
  7.8 2.5 %collective-permute-start = (bf16[2,128,256]{2,1,0:T(8,128)(2,1)S(1)}, bf16[2,128,256]{2,1,0:T(8,128)(2,1)S(1)}, u32[]{:S(2)}, u32[]{:S(2)}) collective-permute-start(bf16[2,128,256]{2,1,0:T(8,128)(2,1)S(1)} %pad_maximum_fusion.1.refs_3_), channel_id=1, source_target_pairs={{0,1},{1,2},{2,3},{3,4},{4,5},{5,6},{6,7},{8,9},{9,10},{10,11},{11... | collective-permute-start | bytes 393224 | tf_op jit(solution)/shard_map/ppermute | solution.py:437
  19.4 3.1 %attend.3 = (f32[2,512,128]{2,1,0:T(8,128)S(1)}, f32[2,512,128]{2,1,0:T(8,128)S(1)}, f32[2,512,128]{2,1,0:T(8,128)S(1)}) custom-call(bf16[2,1024,128]{2,1,0:T(8,128)(2,1)S(1)} %get-tuple-element.61.refs_0_, bf16[2,128,256]{2,1,0:T(8,128)(2,1)S(1)} %collective-permute-done.refs_1_, f32[128,128]{1,0:T(8,128)S(1)} %get-tuple-element.62.refs_2_, ...), custom_call_target="tpu_custom_call" | custom-call | bytes 19250000 | tf_op jit(solution)/shard_map/attend/pallas_call | solution.py:189
  22.6 2.6 %collective-permute-done.4.refs_6_ = bf16[2,256,256]{2,1,0:T(8,128)(2,1)S(1)} collective-permute-done((bf16[2,256,256]{2,1,0:T(8,128)(2,1)S(1)}, bf16[2,256,256]{2,1,0:T(8,128)(2,1)S(1)}, u32[]{:S(2)}, u32[]{:S(2)}) %collective-permute-start.4) | collective-permute-done | bytes 262176 | tf_op jit(solution)/shard_map/ppermute | solution.py:415
  29.0 2.6 %attend.4 = (f32[2,512,128]{2,1,0:T(8,128)S(1)}, f32[2,512,128]{2,1,0:T(8,128)S(1)}, f32[2,512,128]{2,1,0:T(8,128)S(1)}) custom-call(bf16[2,1024,128]{2,1,0:T(8,128)(2,1)S(1)} %get-tuple-element.61.refs_0_, f32[2,512,128]{2,1,0:T(8,128)S(1)} %get-tuple-element.66.refs_1_, f32[2,512,128]{2,1,0:T(8,128)S(1)} %get-tuple-element.67.refs_2_, ...), custom_call_target="tpu_custom_call" | custom-call | bytes 7700000 | tf_op jit(solution)/shard_map/attend/pallas_call | solution.py:189
  31.6 2.5 %collective-permute-done.6.refs_6_ = bf16[2,256,256]{2,1,0:T(8,128)(2,1)S(1)} collective-permute-done((bf16[2,256,256]{2,1,0:T(8,128)(2,1)S(1)}, bf16[2,256,256]{2,1,0:T(8,128)(2,1)S(1)}, u32[]{:S(2)}, u32[]{:S(2)}) %collective-permute-start.6) | collective-permute-done | bytes 262176 | tf_op jit(solution)/shard_map/ppermute | solution.py:415
  38.2 2.6 %attend.5 = (f32[2,512,128]{2,1,0:T(8,128)S(1)}, f32[2,512,128]{2,1,0:T(8,128)S(1)}, f32[2,512,128]{2,1,0:T(8,128)S(1)}) custom-call(bf16[2,1024,128]{2,1,0:T(8,128)(2,1)S(1)} %get-tuple-element.61.refs_0_, f32[2,512,128]{2,1,0:T(8,128)S(1)} %get-tuple-element.70.refs_1_, f32[2,512,128]{2,1,0:T(8,128)S(1)} %get-tuple-element.71.refs_2_, ...), custom_call_target="tpu_custom_call" | custom-call | bytes 7700000 | tf_op jit(solution)/shard_map/attend/pallas_call | solution.py:189
  40.9 4.5 %collective-permute-done.9.refs_4_ = bf16[2,256,256]{2,1,0:T(8,128)(2,1)S(1)} collective-permute-done((bf16[2,256,256]{2,1,0:T(8,128)(2,1)S(1)}, bf16[2,256,256]{2,1,0:T(8,128)(2,1)S(1)}, u32[]{:S(2)}, u32[]{:S(2)}) %collective-permute-start.9) | collective-permute-done | bytes 262176 | tf_op jit(solution)/shard_map/ppermute | solution.py:418
  45.4 2.5 %attend_project.1 = (f32[128,2048]{1,0:T(8,128)S(1)}, bf16[128,1024]{1,0:T(8,128)(2,1)S(1)}, bf16[128,1024]{1,0:T(8,128)(2,1)S(1)}) custom-call(bf16[2,1024,128]{2,1,0:T(8,128)(2,1)S(1)} %get-tuple-element.61.refs_0_, f32[2,512,128]{2,1,0:T(8,128)S(1)} %get-tuple-element.75.refs_1_, f32[2,512,128]{2,1,0:T(8,128)S(1)} %get-tuple-element.76.refs_2_, ...), custom_call_target="tpu_custom_call" | custom-call | bytes 10850000 | tf_op jit(solution)/shard_map/attend_project/pallas_call | solution.py:252
  51.8 9.2 %collective-permute-done.15.refs_10_ = bf16[512,1024]{1,0:T(8,128)(2,1)S(1)} collective-permute-done((bf16[512,1024]{1,0:T(8,128)(2,1)S(1)}, bf16[512,1024]{1,0:T(8,128)(2,1)S(1)}, u32[]{:S(2)}, u32[]{:S(2)}) %collective-permute-start.15) | collective-permute-done | bytes 1048608 | tf_op jit(solution)/shard_map/ppermute | solution.py:423
  61.5 2.7 %collective-permute-done.18.refs_11_ = bf16[512,1024]{1,0:T(8,128)(2,1)S(1)} collective-permute-done((bf16[512,1024]{1,0:T(8,128)(2,1)S(1)}, bf16[512,1024]{1,0:T(8,128)(2,1)S(1)}, u32[]{:S(2)}, u32[]{:S(2)}) %collective-permute-start.18) | collective-permute-done | bytes 1048608 | tf_op jit(solution)/shard_map/ppermute | solution.py:427
  69.8 4.6 %collective-permute-done.20.refs_2_ = bf16[128,1024]{1,0:T(8,128)(2,1)S(1)} collective-permute-done((bf16[128,1024]{1,0:T(8,128)(2,1)S(1)}, bf16[128,1024]{1,0:T(8,128)(2,1)S(1)}, u32[]{:S(2)}, u32[]{:S(2)}) %collective-permute-start.20) | collective-permute-done | bytes 262176 | tf_op jit(solution)/shard_map/ppermute | solution.py:418
  78.6 2.8 %collective-permute-done.22.refs_1_ = bf16[128,1024]{1,0:T(8,128)(2,1)S(1)} collective-permute-done((bf16[128,1024]{1,0:T(8,128)(2,1)S(1)}, bf16[128,1024]{1,0:T(8,128)(2,1)S(1)}, u32[]{:S(2)}, u32[]{:S(2)}) %collective-permute-start.22) | collective-permute-done | bytes 262176 | tf_op jit(solution)/shard_map/ppermute | solution.py:415
  84.2 2.8 %collective-permute-done.21.refs_0_ = bf16[128,1024]{1,0:T(8,128)(2,1)S(1)} collective-permute-done((bf16[128,1024]{1,0:T(8,128)(2,1)S(1)}, bf16[128,1024]{1,0:T(8,128)(2,1)S(1)}, u32[]{:S(2)}, u32[]{:S(2)}) %collective-permute-start.21) | collective-permute-done | bytes 262176 | tf_op jit(solution)/shard_map/ppermute | solution.py:415
  87.0 4.2 %collective-permute-done.24.refs_1_ = bf16[128,1024]{1,0:T(8,128)(2,1)S(1)} collective-permute-done((bf16[128,1024]{1,0:T(8,128)(2,1)S(1)}, bf16[128,1024]{1,0:T(8,128)(2,1)S(1)}, u32[]{:S(2)}, u32[]{:S(2)}) %collective-permute-start.24) | collective-permute-done | bytes 262176 | tf_op jit(solution)/shard_map/ppermute | solution.py:415
  91.2 3.1 %rise.5.refs_0_ = bf16[256,1024]{1,0:T(8,128)(2,1)S(1)} custom-call(bf16[128,1024]{1,0:T(8,128)(2,1)S(1)} %collective-permute-done.16.refs_0_, bf16[128,1024]{1,0:T(8,128)(2,1)S(1)} %collective-permute-done.17.refs_1_, bf16[128,1024]{1,0:T(8,128)(2,1)S(1)} %collective-permute-done.20.refs_2_, bf16[128,1024]{1,0:T(8,128)(2,1)S(1)} %collective-permute-done.23.refs_3_, ...), custom_call_target="tpu_custom_call" | custom-call | bytes 10500000 | tf_op jit(solution)/shard_map/rise/pallas_call | solution.py:299
  103.4 5.6 %collective-permute-done.26.refs_3_ = bf16[128,1024]{1,0:T(8,128)(2,1)S(1)} collective-permute-done((bf16[128,1024]{1,0:T(8,128)(2,1)S(1)}, bf16[128,1024]{1,0:T(8,128)(2,1)S(1)}, u32[]{:S(2)}, u32[]{:S(2)}) %collective-permute-start.26) | collective-permute-done | bytes 262176 | tf_op jit(solution)/shard_map/ppermute | solution.py:418
  109.0 3.1 %rise.7.refs_0_ = bf16[256,1024]{1,0:T(8,128)(2,1)S(1)} custom-call(bf16[128,1024]{1,0:T(8,128)(2,1)S(1)} %collective-permute-done.19.refs_0_, bf16[128,1024]{1,0:T(8,128)(2,1)S(1)} %collective-permute-done.22.refs_1_, bf16[128,1024]{1,0:T(8,128)(2,1)S(1)} %collective-permute-done.28.refs_2_, bf16[128,1024]{1,0:T(8,128)(2,1)S(1)} %collective-permute-done.29.refs_3_, ...), custom_call_target="tpu_custom_call" | custom-call | bytes 10500000 | tf_op jit(solution)/shard_map/rise/pallas_call | solution.py:299
  114.7 2.5 %collective-permute-start.32 = (bf16[128,1024]{1,0:T(8,128)(2,1)S(1)}, bf16[128,1024]{1,0:T(8,128)(2,1)S(1)}, u32[]{:S(2)}, u32[]{:S(2)}) collective-permute-start(bf16[128,1024]{1,0:T(8,128)(2,1)S(1)} %add_convert_fusion.5), channel_id=1, source_target_pairs={{0,4},{1,5},{4,6},{5,7},{6,2},{7,3},{2,0},{3,1},{8,12},{9,13},{12,... | collective-permute-start | bytes 786440 | tf_op jit(solution)/shard_map/ppermute | solution.py:415
  120.3 2.5 %collective-permute-start.41 = (bf16[128,1024]{1,0:T(8,128)(2,1)S(1)}, bf16[128,1024]{1,0:T(8,128)(2,1)S(1)}, u32[]{:S(2)}, u32[]{:S(2)}) collective-permute-start(bf16[128,1024]{1,0:T(8,128)(2,1)S(1)} %add_convert_fusion.2), channel_id=1, source_target_pairs={{0,4},{1,5},{4,6},{5,7},{6,2},{7,3},{2,0},{3,1},{8,12},{9,13},{12,... | collective-permute-start | bytes 786440 | tf_op jit(solution)/shard_map/ppermute | solution.py:415
  122.8 3.0 %rise.6.refs_0_ = bf16[256,1024]{1,0:T(8,128)(2,1)S(1)} custom-call(bf16[128,1024]{1,0:T(8,128)(2,1)S(1)} %collective-permute-done.21.refs_0_, bf16[128,1024]{1,0:T(8,128)(2,1)S(1)} %collective-permute-done.24.refs_1_, bf16[128,1024]{1,0:T(8,128)(2,1)S(1)} %collective-permute-done.25.refs_2_, bf16[128,1024]{1,0:T(8,128)(2,1)S(1)} %collective-permute-done.26.refs_3_, ...), custom_call_target="tpu_custom_call" | custom-call | bytes 10500000 | tf_op jit(solution)/shard_map/rise/pallas_call | solution.py:299
  134.1 3.1 %rise.4.refs_0_ = bf16[256,1024]{1,0:T(8,128)(2,1)S(1)} custom-call(bf16[128,1024]{1,0:T(8,128)(2,1)S(1)} %get-tuple-element.83.refs_0_, bf16[128,1024]{1,0:T(8,128)(2,1)S(1)} %get-tuple-element.84.refs_1_, bf16[128,1024]{1,0:T(8,128)(2,1)S(1)} %collective-permute-done.13.refs_2_, bf16[128,1024]{1,0:T(8,128)(2,1)S(1)} %collective-permute-done.14.refs_3_, ...), custom_call_target="tpu_custom_call" | custom-call | bytes 10500000 | tf_op jit(solution)/shard_map/rise/pallas_call | solution.py:299
  145.8 3.2 %collective-permute-done.34.refs_1_ = bf16[128,1024]{1,0:T(8,128)(2,1)S(1)} collective-permute-done((bf16[128,1024]{1,0:T(8,128)(2,1)S(1)}, bf16[128,1024]{1,0:T(8,128)(2,1)S(1)}, u32[]{:S(2)}, u32[]{:S(2)}) %collective-permute-start.34) | collective-permute-done | bytes 262176 | tf_op jit(solution)/shard_map/ppermute | solution.py:507
  149.0 4.6 %collective-permute-done.43.refs_4_ = bf16[128,1024]{1,0:T(8,128)(2,1)S(1)} collective-permute-done((bf16[128,1024]{1,0:T(8,128)(2,1)S(1)}, bf16[128,1024]{1,0:T(8,128)(2,1)S(1)}, u32[]{:S(2)}, u32[]{:S(2)}) %collective-permute-start.43) | collective-permute-done | bytes 262176 | tf_op jit(solution)/shard_map/ppermute | solution.py:507
  (112 shorter events, 70.5 us)
Async XLA Ops:
  1.1 15.2 %collective-permute-start.2 = (bf16[2,256,256]{2,1,0:T(8,128)(2,1)S(1)}, bf16[2,256,256]{2,1,0:T(8,128)(2,1)S(1)}, u32[]{:S(2)}, u32[]{:S(2)}) collective-permute-start(bf16[2,256,256]{2,1,0:T(8,128)(2,1)S(1)} %pad_maximum_fusion.refs_5_), channel_id=1, source_target_pairs={{0,4},{1,5},{4,6},{5,7},{6,2},{7,3},{2,0},{3,1},{8,12},{9,13},{12,... | collective-permute-start | bytes 786440 | tf_op jit(solution)/shard_map/ppermute | solution.py:415
  5.2 11.2 %collective-permute-start.1 = (bf16[2,256,256]{2,1,0:T(8,128)(2,1)S(1)}, bf16[2,256,256]{2,1,0:T(8,128)(2,1)S(1)}, u32[]{:S(2)}, u32[]{:S(2)}) collective-permute-start(bf16[2,256,256]{2,1,0:T(8,128)(2,1)S(1)} %pad_maximum_fusion.refs_5_), channel_id=1, source_target_pairs={{0,1},{1,0},{4,5},{5,4},{6,7},{7,6},{2,3},{3,2},{8,9},{9,8},{12,13... | collective-permute-start | bytes 786440 | tf_op jit(solution)/shard_map/ppermute | solution.py:418
  10.4 24.9 %collective-permute-start.8 = (bf16[512,1024]{1,0:T(8,128)(2,1)}, bf16[512,1024]{1,0:T(8,128)(2,1)S(1)}, u32[]{:S(2)}, u32[]{:S(2)}) collective-permute-start(bf16[512,1024]{1,0:T(8,128)(2,1)} %refs_4_.7), channel_id=1, source_target_pairs={{0,16},{8,24},{16,0},{24,8},{1,17},{9,25},{17,1},{25,9},{2,18},{10... | collective-permute-start | bytes 3145736 | tf_op jit(solution)/shard_map/ppermute | solution.py:423
  16.4 18.9 %collective-permute-start.7 = (bf16[512,1024]{1,0:T(8,128)(2,1)}, bf16[512,1024]{1,0:T(8,128)(2,1)S(1)}, u32[]{:S(2)}, u32[]{:S(2)}) collective-permute-start(bf16[512,1024]{1,0:T(8,128)(2,1)} %refs_4_.7), channel_id=1, source_target_pairs={{0,8},{8,0},{16,24},{24,16},{1,9},{9,1},{17,25},{25,17},{2,10},{10... | collective-permute-start | bytes 3145736 | tf_op jit(solution)/shard_map/ppermute | solution.py:427
  29.0 11.9 %collective-permute-start.10 = (bf16[512,1024]{1,0:T(8,128)(2,1)}, bf16[512,1024]{1,0:T(8,128)(2,1)S(1)}, u32[]{:S(2)}, u32[]{:S(2)}) collective-permute-start(bf16[512,1024]{1,0:T(8,128)(2,1)} %refs_8_.7), channel_id=1, source_target_pairs={{0,8},{8,0},{16,24},{24,16},{1,9},{9,1},{17,25},{25,17},{2,10},{10... | collective-permute-start | bytes 3145736 | tf_op jit(solution)/shard_map/ppermute | solution.py:427
  35.9 25.1 %collective-permute-start.15 = (bf16[512,1024]{1,0:T(8,128)(2,1)S(1)}, bf16[512,1024]{1,0:T(8,128)(2,1)S(1)}, u32[]{:S(2)}, u32[]{:S(2)}) collective-permute-start(bf16[512,1024]{1,0:T(8,128)(2,1)S(1)} %copy-done.1), channel_id=1, source_target_pairs={{0,16},{8,24},{16,0},{24,8},{1,17},{9,25},{17,1},{25,9},{2,18},{10... | collective-permute-start | bytes 3145736 | tf_op jit(solution)/shard_map/ppermute | solution.py:423
  47.8 13.2 %collective-permute-start.16 = (bf16[128,1024]{1,0:T(8,128)(2,1)S(1)}, bf16[128,1024]{1,0:T(8,128)(2,1)S(1)}, u32[]{:S(2)}, u32[]{:S(2)}) collective-permute-start(bf16[128,1024]{1,0:T(8,128)(2,1)S(1)} %get-tuple-element.83.refs_0_), channel_id=1, source_target_pairs={{0,4},{1,5},{4,6},{5,7},{6,2},{7,3},{2,0},{3,1},{8,12},{9,13},{12,... | collective-permute-start | bytes 786440 | tf_op jit(solution)/shard_map/ppermute | solution.py:415
  49.1 12.0 %collective-permute-start.13 = (bf16[128,1024]{1,0:T(8,128)(2,1)S(1)}, bf16[128,1024]{1,0:T(8,128)(2,1)S(1)}, u32[]{:S(2)}, u32[]{:S(2)}) collective-permute-start(bf16[128,1024]{1,0:T(8,128)(2,1)S(1)} %get-tuple-element.83.refs_0_), channel_id=1, source_target_pairs={{0,1},{1,0},{4,5},{5,4},{6,7},{7,6},{2,3},{3,2},{8,9},{9,8},{12,13... | collective-permute-start | bytes 786440 | tf_op jit(solution)/shard_map/ppermute | solution.py:418
  50.1 10.9 %collective-permute-start.17 = (bf16[128,1024]{1,0:T(8,128)(2,1)S(1)}, bf16[128,1024]{1,0:T(8,128)(2,1)S(1)}, u32[]{:S(2)}, u32[]{:S(2)}) collective-permute-start(bf16[128,1024]{1,0:T(8,128)(2,1)S(1)} %get-tuple-element.84.refs_1_), channel_id=1, source_target_pairs={{0,4},{1,5},{4,6},{5,7},{6,2},{7,3},{2,0},{3,1},{8,12},{9,13},{12,... | collective-permute-start | bytes 786440 | tf_op jit(solution)/shard_map/ppermute | solution.py:415
  64.2 26.9 %collective-permute-start.36 = (bf16[1024,512]{1,0:T(8,128)(2,1)S(1)}, bf16[1024,512]{1,0:T(8,128)(2,1)S(1)}, u32[]{:S(2)}, u32[]{:S(2)}) collective-permute-start(bf16[1024,512]{1,0:T(8,128)(2,1)S(1)} %copy-done.2), channel_id=1, source_target_pairs={{0,16},{8,24},{16,0},{24,8},{1,17},{9,25},{17,1},{25,9},{2,18},{10... | collective-permute-start | bytes 3145736 | tf_op jit(solution)/shard_map/ppermute | solution.py:423
  68.0 13.3 %collective-permute-start.22 = (bf16[128,1024]{1,0:T(8,128)(2,1)S(1)}, bf16[128,1024]{1,0:T(8,128)(2,1)S(1)}, u32[]{:S(2)}, u32[]{:S(2)}) collective-permute-start(bf16[128,1024]{1,0:T(8,128)(2,1)S(1)} %collective-permute-done.17.refs_1_), channel_id=1, source_target_pairs={{0,4},{1,5},{4,6},{5,7},{6,2},{7,3},{2,0},{3,1},{8,12},{9,13},{12,... | collective-permute-start | bytes 786440 | tf_op jit(solution)/shard_map/ppermute | solution.py:415
  69.2 12.2 %collective-permute-start.23 = (bf16[128,1024]{1,0:T(8,128)(2,1)S(1)}, bf16[128,1024]{1,0:T(8,128)(2,1)S(1)}, u32[]{:S(2)}, u32[]{:S(2)}) collective-permute-start(bf16[128,1024]{1,0:T(8,128)(2,1)S(1)} %collective-permute-done.17.refs_1_), channel_id=1, source_target_pairs={{0,1},{1,0},{4,5},{5,4},{6,7},{7,6},{2,3},{3,2},{8,9},{9,8},{12,13... | collective-permute-start | bytes 786440 | tf_op jit(solution)/shard_map/ppermute | solution.py:418
  75.7 11.2 %collective-permute-start.21 = (bf16[128,1024]{1,0:T(8,128)(2,1)S(1)}, bf16[128,1024]{1,0:T(8,128)(2,1)S(1)}, u32[]{:S(2)}, u32[]{:S(2)}) collective-permute-start(bf16[128,1024]{1,0:T(8,128)(2,1)S(1)} %collective-permute-done.19.refs_0_), channel_id=1, source_target_pairs={{0,4},{1,5},{4,6},{5,7},{6,2},{7,3},{2,0},{3,1},{8,12},{9,13},{12,... | collective-permute-start | bytes 786440 | tf_op jit(solution)/shard_map/ppermute | solution.py:415
  95.1 14.0 %collective-permute-start.26 = (bf16[128,1024]{1,0:T(8,128)(2,1)S(1)}, bf16[128,1024]{1,0:T(8,128)(2,1)S(1)}, u32[]{:S(2)}, u32[]{:S(2)}) collective-permute-start(bf16[128,1024]{1,0:T(8,128)(2,1)S(1)} %collective-permute-done.24.refs_1_), channel_id=1, source_target_pairs={{0,1},{1,0},{4,5},{5,4},{6,7},{7,6},{2,3},{3,2},{8,9},{9,8},{12,13... | collective-permute-start | bytes 786440 | tf_op jit(solution)/shard_map/ppermute | solution.py:418
  97.6 17.1 %collective-permute-start.31 = (bf16[128,1024]{1,0:T(8,128)(2,1)S(1)}, bf16[128,1024]{1,0:T(8,128)(2,1)S(1)}, u32[]{:S(2)}, u32[]{:S(2)}) collective-permute-start(bf16[128,1024]{1,0:T(8,128)(2,1)S(1)} %get-tuple-element.104), channel_id=1, source_target_pairs={{0,1},{1,0},{4,5},{5,4},{6,7},{7,6},{2,3},{3,2},{8,9},{9,8},{12,13... | collective-permute-start | bytes 786440 | tf_op jit(solution)/shard_map/ppermute | solution.py:507
  99.6 20.6 %collective-permute-start.40 = (bf16[128,1024]{1,0:T(8,128)(2,1)S(1)}, bf16[128,1024]{1,0:T(8,128)(2,1)S(1)}, u32[]{:S(2)}, u32[]{:S(2)}) collective-permute-start(bf16[128,1024]{1,0:T(8,128)(2,1)S(1)} %get-tuple-element.115), channel_id=1, source_target_pairs={{0,1},{1,0},{4,5},{5,4},{6,7},{7,6},{2,3},{3,2},{8,9},{9,8},{12,13... | collective-permute-start | bytes 786440 | tf_op jit(solution)/shard_map/ppermute | solution.py:507
  113.3 14.3 %collective-permute-start.30 = (bf16[128,1024]{1,0:T(8,128)(2,1)S(1)}, bf16[128,1024]{1,0:T(8,128)(2,1)S(1)}, u32[]{:S(2)}, u32[]{:S(2)}) collective-permute-start(bf16[128,1024]{1,0:T(8,128)(2,1)S(1)} %get-tuple-element.102), channel_id=1, source_target_pairs={{0,1},{1,0},{4,5},{5,4},{6,7},{7,6},{2,3},{3,2},{8,9},{9,8},{12,13... | collective-permute-start | bytes 786440 | tf_op jit(solution)/shard_map/ppermute | solution.py:507
  114.7 12.9 %collective-permute-start.32 = (bf16[128,1024]{1,0:T(8,128)(2,1)S(1)}, bf16[128,1024]{1,0:T(8,128)(2,1)S(1)}, u32[]{:S(2)}, u32[]{:S(2)}) collective-permute-start(bf16[128,1024]{1,0:T(8,128)(2,1)S(1)} %add_convert_fusion.5), channel_id=1, source_target_pairs={{0,4},{1,5},{4,6},{5,7},{6,2},{7,3},{2,0},{3,1},{8,12},{9,13},{12,... | collective-permute-start | bytes 786440 | tf_op jit(solution)/shard_map/ppermute | solution.py:415
  118.4 13.1 %collective-permute-start.39 = (bf16[128,1024]{1,0:T(8,128)(2,1)S(1)}, bf16[128,1024]{1,0:T(8,128)(2,1)S(1)}, u32[]{:S(2)}, u32[]{:S(2)}) collective-permute-start(bf16[128,1024]{1,0:T(8,128)(2,1)S(1)} %get-tuple-element.113), channel_id=1, source_target_pairs={{0,1},{1,0},{4,5},{5,4},{6,7},{7,6},{2,3},{3,2},{8,9},{9,8},{12,13... | collective-permute-start | bytes 786440 | tf_op jit(solution)/shard_map/ppermute | solution.py:507
  120.3 11.2 %collective-permute-start.41 = (bf16[128,1024]{1,0:T(8,128)(2,1)S(1)}, bf16[128,1024]{1,0:T(8,128)(2,1)S(1)}, u32[]{:S(2)}, u32[]{:S(2)}) collective-permute-start(bf16[128,1024]{1,0:T(8,128)(2,1)S(1)} %add_convert_fusion.2), channel_id=1, source_target_pairs={{0,4},{1,5},{4,6},{5,7},{6,2},{7,3},{2,0},{3,1},{8,12},{9,13},{12,... | collective-permute-start | bytes 786440 | tf_op jit(solution)/shard_map/ppermute | solution.py:415
  127.1 11.3 %collective-permute-start.27 = (bf16[128,1024]{1,0:T(8,128)(2,1)S(1)}, bf16[128,1024]{1,0:T(8,128)(2,1)S(1)}, u32[]{:S(2)}, u32[]{:S(2)}) collective-permute-start(bf16[128,1024]{1,0:T(8,128)(2,1)S(1)} %get-tuple-element.96), channel_id=1, source_target_pairs={{0,1},{1,0},{4,5},{5,4},{6,7},{7,6},{2,3},{3,2},{8,9},{9,8},{12,13... | collective-permute-start | bytes 786440 | tf_op jit(solution)/shard_map/ppermute | solution.py:507
  129.7 13.0 %collective-permute-start.38 = (bf16[128,1024]{1,0:T(8,128)(2,1)S(1)}, bf16[128,1024]{1,0:T(8,128)(2,1)S(1)}, u32[]{:S(2)}, u32[]{:S(2)}) collective-permute-start(bf16[128,1024]{1,0:T(8,128)(2,1)S(1)} %get-tuple-element.111), channel_id=1, source_target_pairs={{0,1},{1,0},{4,5},{5,4},{6,7},{7,6},{2,3},{3,2},{8,9},{9,8},{12,13... | collective-permute-start | bytes 786440 | tf_op jit(solution)/shard_map/ppermute | solution.py:507
  131.6 11.1 %collective-permute-start.42 = (bf16[128,1024]{1,0:T(8,128)(2,1)S(1)}, bf16[128,1024]{1,0:T(8,128)(2,1)S(1)}, u32[]{:S(2)}, u32[]{:S(2)}) collective-permute-start(bf16[128,1024]{1,0:T(8,128)(2,1)S(1)} %add_convert_fusion.1), channel_id=1, source_target_pairs={{0,4},{1,5},{4,6},{5,7},{6,2},{7,3},{2,0},{3,1},{8,12},{9,13},{12,... | collective-permute-start | bytes 786440 | tf_op jit(solution)/shard_map/ppermute | solution.py:415
  142.9 10.7 %collective-permute-start.43 = (bf16[128,1024]{1,0:T(8,128)(2,1)S(1)}, bf16[128,1024]{1,0:T(8,128)(2,1)S(1)}, u32[]{:S(2)}, u32[]{:S(2)}) collective-permute-start(bf16[128,1024]{1,0:T(8,128)(2,1)S(1)} %get-tuple-element.116), channel_id=1, source_target_pairs={{0,1},{1,0},{4,5},{5,4},{6,7},{7,6},{2,3},{3,2},{8,9},{9,8},{12,13... | collective-permute-start | bytes 786440 | tf_op jit(solution)/shard_map/ppermute | solution.py:507
  (31 other events, 405.8 us)
where the time goes:
time: 155 us
  waiting for transfers between devices  59.4 us (38%)
  starting transfers between devices  53.7 us (35%)
  Pallas kernels  35.5 us (23%)
  local copies, waits for them, and re-layouts  2.94 us (2%)
  other arithmetic  2.8 us (2%)
    ppermute x15, starting transfers between devices, round_z(): return lax.ppermute(tie(block, *others), 'dev', shift(1, 0))  28.2 us
    ppermute x12, waiting for transfers between devices, along_y(): lax.ppermute(tie(block, *others), 'dev', shift(0, ys))  20.3 us
    ppermute x15, waiting for transfers between devices, round_z(): return lax.ppermute(tie(block, *others), 'dev', shift(1, 0))  16.1 us
    pallas_call x4, Pallas kernels, rise(): pl.pallas_call(kernel, out_shape=jax.ShapeDtypeStruct((parts * tokens, hi...  12.3 us
    ppermute x12, starting transfers between devices, along_y(): lax.ppermute(tie(block, *others), 'dev', shift(0, ys))  11.3 us
    ppermute x8, waiting for transfers between devices, shards(): lax.ppermute(parts[ys], 'dev', shift(0, -ys))  11.1 us
    pallas_call x8, Pallas kernels, fall(): pl.pallas_call(kernel, out_shape=[shape] * parts, in_specs=[vmem] * (1 +...  9.8 us
    ppermute x3, waiting for transfers between devices, along_x(): blocks.append(lax.ppermute(tie(blocks[-1], *others), 'grp', x_shift))  9.17 us
  transfers between devices with their start and end apart: 45, of which 21 were waited for; matrix products, arithmetic and copies ran while one was open for 1% of the time, Pallas kernels for 22%

commit v1 on v0

--- a/solution.py
+++ b/solution.py
@@ -446,7 +446,7 @@
         width,
     )
     blocks = [(before, before_mask), (own, within_mask), (prefix, prefix_mask)]
-    ready, state = [q, before], None
+    ready, state = [], None
     for zs in range(1, depth_z):
         if zs == depth_z - 1:
             ready += [gate_swap, *gate_rows[1:]]
@@ -479,28 +479,40 @@
     arrived, across = [normed], [[along_y(half) for half in normed]]
     ups, downs, acts = [w_up, up_swap], [w_down, down_swap], {}
     for zs in range(1, depth_z):
-        waits = across[zs - 2] if zs > 1 else [[] for _ in normed]
+        before = [b for c in across[zs - 2] for b in c] if zs > 1 else []
+        waits = [before for _ in normed]
+        if zs == depth_z - 1:
+            down_cols = along_x(w_down, *ups[3:], *arrived[2], *[b for c in across[1] for b in c])
+        if zs == depth_z - 1:
+            acts[1] = rise([arrived[1]] + [list(c) for c in zip(*across[1])], gates, ups)
+            acts[0] = rise([arrived[0]] + [list(c) for c in zip(*across[0])], gates, ups)
         arrived.append([round_z(half, *wait) for half, wait in zip(arrived[-1], waits)])
         if zs == 1:
             for up in up_rows[1:]:
                 ups += [up, other_core(up, *arrived[1], *[b for c in across[0] for b in c])]
-            down_cols = along_x(w_down, *ups[3:])
-        late = arrived[zs - 1][1:] if zs > 1 else []
+        late = arrived[zs][1:] + [b for c in across[-1] for b in c]
         if zs == depth_z - 1:
-            acts[1] = rise([arrived[1]] + [list(c) for c in zip(*across[1])], gates, ups)
-            late = [*late, acts[1]]
+            late += [acts[1]]
         across.append([along_y(half, *late) for half in arrived[zs]])
     chunks = [[a] + [list(c) for c in zip(*b)] for a, b in zip(arrived, across)]
+    each = grps // HALVES
+    fallen = {}
+    acts[2] = rise(chunks[2], gates, ups)
+    soon = [b for c in across[-1] for b in c] + [acts[2]]
+    if each <= len(downs):
+        fallen[1, 0] = fall(acts[1], depth_y, downs[:each])
+        soon.append(fallen[1, 0][0])
     for down in down_cols[1:]:
-        downs += [down, other_core(down, *arrived[-1], *[b for c in across[-2] for b in c])]
-    chunks[2][0] = [tie(half, *[b for c in across[-1] for b in c]) for half in chunks[2][0]]
+        downs += [down, other_core(down, *soon)]
 
     running, terms = [None] * HALVES, [None] * HALVES
-    each = len(downs) // HALVES
     for zs in list(range(1, depth_z)) + [0]:
         act = acts[zs] if zs in acts else rise(chunks[zs], gates, ups)
         for half in range(HALVES):
-            parts = fall(act, depth_y, downs[half * each : (half + 1) * each])
+            if (zs, half) in fallen:
+                parts = fallen[zs, half]
+            else:
+                parts = fall(act, depth_y, downs[half * each : (half + 1) * each])
             if zs == 0:
                 parts = [parts[0]] + [tie(part, running[half]) for part in parts[1:]]
             terms[half] = [parts[0]] + [

time: 155 us -> 157 us (1.013)
  waiting for transfers between devices: 59.4 us -> 66.9 us
  starting transfers between devices: 53.7 us -> 48 us
    ppermute x12, waiting for transfers between devices: 20.3 us -> 26.3 us  [along_y(): lax.ppermute(tie(block, *others), 'dev', shift(0, ys))]
    ppermute x15, starting transfers between devices: 28.2 us -> 22.2 us  [round_z(): return lax.ppermute(tie(block, *others), 'dev', shift(1, 0))]
    ppermute x8, waiting for transfers between devices: 11.1 us -> 15.6 us  [shards(): lax.ppermute(parts[ys], 'dev', shift(0, -ys))]
    ppermute x15, waiting for transfers between devices: 16.1 us -> 13 us  [round_z(): return lax.ppermute(tie(block, *others), 'dev', shift(1, 0))]
  transfers between devices with their start and end apart: 45 -> 45, of which waited for: 21 -> 23; matrix products, arithmetic and copies ran while one was open for 1% -> 1% of each run, Pallas kernels for 22% -> 22%
where the time goes in v1:
time: 157 us
  waiting for transfers between devices  66.9 us (43%)
  starting transfers between devices  48 us (31%)
  Pallas kernels  35.5 us (23%)
  local copies, waits for them, and re-layouts  2.93 us (2%)
  other arithmetic  2.8 us (2%)
    ppermute x12, waiting for transfers between devices, along_y(): lax.ppermute(tie(block, *others), 'dev', shift(0, ys))  26.3 us
    ppermute x15, starting transfers between devices, round_z(): return lax.ppermute(tie(block, *others), 'dev', shift(1, 0))  22.2 us
    ppermute x8, waiting for transfers between devices, shards(): lax.ppermute(parts[ys], 'dev', shift(0, -ys))  15.6 us
    ppermute x15, waiting for transfers between devices, round_z(): return lax.ppermute(tie(block, *others), 'dev', shift(1, 0))  13 us
    pallas_call x4, Pallas kernels, rise(): pl.pallas_call(kernel, out_shape=jax.ShapeDtypeStruct((parts * tokens, hi...  12.3 us
    ppermute x12, starting transfers between devices, along_y(): lax.ppermute(tie(block, *others), 'dev', shift(0, ys))  11.3 us
    pallas_call x8, Pallas kernels, fall(): pl.pallas_call(kernel, out_shape=[shape] * parts, in_specs=[vmem] * (1 +...  9.81 us
    ppermute x3, waiting for transfers between devices, along_x(): blocks.append(lax.ppermute(tie(blocks[-1], *others), 'grp', x_shift))  9.33 us
  transfers between devices with their start and end apart: 45, of which 23 were waited for; matrix products, arithmetic and copies ran while one was open for 1% of the time, Pallas kernels for 22%

profile of v1, /device:TPU:0, one launch (start us, length us, event | category | flops | bytes accessed | tf_op | source)
XLA Modules:
  0.0 156.5 jit_solution(17091429058524069836)
XLA Ops:
  1.1 4.1 %collective-permute-start.2 = (bf16[2,256,256]{2,1,0:T(8,128)(2,1)S(1)}, bf16[2,256,256]{2,1,0:T(8,128)(2,1)S(1)}, u32[]{:S(2)}, u32[]{:S(2)}) collective-permute-start(bf16[2,256,256]{2,1,0:T(8,128)(2,1)S(1)} %pad_maximum_fusion.refs_5_), channel_id=1, source_target_pairs={{0,4},{1,5},{4,6},{5,7},{6,2},{7,3},{2,0},{3,1},{8,12},{9,13},{12,... | collective-permute-start | bytes 786440 | tf_op jit(solution)/shard_map/ppermute | solution.py:415
  8.3 2.6 %collective-permute-done.2.refs_9_ = bf16[2,256,256]{2,1,0:T(8,128)(2,1)S(1)} collective-permute-done((bf16[2,256,256]{2,1,0:T(8,128)(2,1)S(1)}, bf16[2,256,256]{2,1,0:T(8,128)(2,1)S(1)}, u32[]{:S(2)}, u32[]{:S(2)}) %collective-permute-start.2) | collective-permute-done | bytes 262176 | tf_op jit(solution)/shard_map/ppermute | solution.py:415
  10.8 2.2 %collective-permute-done.1.refs_7_ = bf16[2,256,256]{2,1,0:T(8,128)(2,1)S(1)} collective-permute-done((bf16[2,256,256]{2,1,0:T(8,128)(2,1)S(1)}, bf16[2,256,256]{2,1,0:T(8,128)(2,1)S(1)}, u32[]{:S(2)}, u32[]{:S(2)}) %collective-permute-start.1) | collective-permute-done | bytes 262176 | tf_op jit(solution)/shard_map/ppermute | solution.py:418
  17.1 2.5 %collective-permute-start = (bf16[2,128,256]{2,1,0:T(8,128)(2,1)S(1)}, bf16[2,128,256]{2,1,0:T(8,128)(2,1)S(1)}, u32[]{:S(2)}, u32[]{:S(2)}) collective-permute-start(bf16[2,128,256]{2,1,0:T(8,128)(2,1)S(1)} %pad_maximum_fusion.1.refs_3_), channel_id=1, source_target_pairs={{0,1},{1,2},{2,3},{3,4},{4,5},{5,6},{6,7},{8,9},{9,10},{10,11},{11... | collective-permute-start | bytes 393224 | tf_op jit(solution)/shard_map/ppermute | solution.py:437
  24.9 3.1 %attend.3 = (f32[2,512,128]{2,1,0:T(8,128)S(1)}, f32[2,512,128]{2,1,0:T(8,128)S(1)}, f32[2,512,128]{2,1,0:T(8,128)S(1)}) custom-call(bf16[2,1024,128]{2,1,0:T(8,128)(2,1)S(1)} %get-tuple-element.61.refs_0_, bf16[2,128,256]{2,1,0:T(8,128)(2,1)S(1)} %collective-permute-done.refs_1_, f32[128,128]{1,0:T(8,128)S(1)} %get-tuple-element.62.refs_2_, ...), custom_call_target="tpu_custom_call" | custom-call | bytes 19250000 | tf_op jit(solution)/shard_map/attend/pallas_call | solution.py:189
  28.0 3.1 %collective-permute-start.6 = (bf16[2,256,256]{2,1,0:T(8,128)(2,1)S(1)}, bf16[2,256,256]{2,1,0:T(8,128)(2,1)S(1)}, u32[]{:S(2)}, u32[]{:S(2)}) collective-permute-start(bf16[2,256,256]{2,1,0:T(8,128)(2,1)S(1)} %collective-permute-done.4.refs_6_), channel_id=1, source_target_pairs={{0,4},{1,5},{4,6},{5,7},{6,2},{7,3},{2,0},{3,1},{8,12},{9,13},{12,... | collective-permute-start | bytes 786440 | tf_op jit(solution)/shard_map/ppermute | solution.py:415
  31.2 2.6 %attend.4 = (f32[2,512,128]{2,1,0:T(8,128)S(1)}, f32[2,512,128]{2,1,0:T(8,128)S(1)}, f32[2,512,128]{2,1,0:T(8,128)S(1)}) custom-call(bf16[2,1024,128]{2,1,0:T(8,128)(2,1)S(1)} %get-tuple-element.61.refs_0_, f32[2,512,128]{2,1,0:T(8,128)S(1)} %get-tuple-element.66.refs_1_, f32[2,512,128]{2,1,0:T(8,128)S(1)} %get-tuple-element.67.refs_2_, ...), custom_call_target="tpu_custom_call" | custom-call | bytes 7700000 | tf_op jit(solution)/shard_map/attend/pallas_call | solution.py:189
  33.8 3.1 %collective-permute-done.6.refs_6_ = bf16[2,256,256]{2,1,0:T(8,128)(2,1)S(1)} collective-permute-done((bf16[2,256,256]{2,1,0:T(8,128)(2,1)S(1)}, bf16[2,256,256]{2,1,0:T(8,128)(2,1)S(1)}, u32[]{:S(2)}, u32[]{:S(2)}) %collective-permute-start.6) | collective-permute-done | bytes 262176 | tf_op jit(solution)/shard_map/ppermute | solution.py:415
  36.9 2.2 %collective-permute-done.5.refs_4_ = bf16[2,256,256]{2,1,0:T(8,128)(2,1)S(1)} collective-permute-done((bf16[2,256,256]{2,1,0:T(8,128)(2,1)S(1)}, bf16[2,256,256]{2,1,0:T(8,128)(2,1)S(1)}, u32[]{:S(2)}, u32[]{:S(2)}) %collective-permute-start.5) | collective-permute-done | bytes 262176 | tf_op jit(solution)/shard_map/ppermute | solution.py:418
  41.5 2.6 %attend.5 = (f32[2,512,128]{2,1,0:T(8,128)S(1)}, f32[2,512,128]{2,1,0:T(8,128)S(1)}, f32[2,512,128]{2,1,0:T(8,128)S(1)}) custom-call(bf16[2,1024,128]{2,1,0:T(8,128)(2,1)S(1)} %get-tuple-element.61.refs_0_, f32[2,512,128]{2,1,0:T(8,128)S(1)} %get-tuple-element.70.refs_1_, f32[2,512,128]{2,1,0:T(8,128)S(1)} %get-tuple-element.71.refs_2_, ...), custom_call_target="tpu_custom_call" | custom-call | bytes 7700000 | tf_op jit(solution)/shard_map/attend/pallas_call | solution.py:189
  44.1 5.1 %collective-permute-done.9.refs_4_ = bf16[2,256,256]{2,1,0:T(8,128)(2,1)S(1)} collective-permute-done((bf16[2,256,256]{2,1,0:T(8,128)(2,1)S(1)}, bf16[2,256,256]{2,1,0:T(8,128)(2,1)S(1)}, u32[]{:S(2)}, u32[]{:S(2)}) %collective-permute-start.9) | collective-permute-done | bytes 262176 | tf_op jit(solution)/shard_map/ppermute | solution.py:418
  49.2 2.5 %attend_project.1 = (f32[128,2048]{1,0:T(8,128)S(1)}, bf16[128,1024]{1,0:T(8,128)(2,1)S(1)}, bf16[128,1024]{1,0:T(8,128)(2,1)S(1)}) custom-call(bf16[2,1024,128]{2,1,0:T(8,128)(2,1)S(1)} %get-tuple-element.61.refs_0_, f32[2,512,128]{2,1,0:T(8,128)S(1)} %get-tuple-element.75.refs_1_, f32[2,512,128]{2,1,0:T(8,128)S(1)} %get-tuple-element.76.refs_2_, ...), custom_call_target="tpu_custom_call" | custom-call | bytes 10850000 | tf_op jit(solution)/shard_map/attend_project/pallas_call | solution.py:252
  55.5 9.3 %collective-permute-done.15.refs_10_ = bf16[512,1024]{1,0:T(8,128)(2,1)S(1)} collective-permute-done((bf16[512,1024]{1,0:T(8,128)(2,1)S(1)}, bf16[512,1024]{1,0:T(8,128)(2,1)S(1)}, u32[]{:S(2)}, u32[]{:S(2)}) %collective-permute-start.15) | collective-permute-done | bytes 1048608 | tf_op jit(solution)/shard_map/ppermute | solution.py:423
  69.2 5.3 %collective-permute-done.19.refs_0_ = bf16[128,1024]{1,0:T(8,128)(2,1)S(1)} collective-permute-done((bf16[128,1024]{1,0:T(8,128)(2,1)S(1)}, bf16[128,1024]{1,0:T(8,128)(2,1)S(1)}, u32[]{:S(2)}, u32[]{:S(2)}) %collective-permute-start.19) | collective-permute-done | bytes 262176 | tf_op jit(solution)/shard_map/ppermute | solution.py:415
  75.7 4.9 %collective-permute-done.21.refs_3_ = bf16[128,1024]{1,0:T(8,128)(2,1)S(1)} collective-permute-done((bf16[128,1024]{1,0:T(8,128)(2,1)S(1)}, bf16[128,1024]{1,0:T(8,128)(2,1)S(1)}, u32[]{:S(2)}, u32[]{:S(2)}) %collective-permute-start.21) | collective-permute-done | bytes 262176 | tf_op jit(solution)/shard_map/ppermute | solution.py:418
  85.8 3.1 %rise.5.refs_0_ = bf16[256,1024]{1,0:T(8,128)(2,1)S(1)} custom-call(bf16[128,1024]{1,0:T(8,128)(2,1)S(1)} %collective-permute-done.16.refs_0_, bf16[128,1024]{1,0:T(8,128)(2,1)S(1)} %collective-permute-done.17.refs_1_, bf16[128,1024]{1,0:T(8,128)(2,1)S(1)} %collective-permute-done.20.refs_2_, bf16[128,1024]{1,0:T(8,128)(2,1)S(1)} %collective-permute-done.21.refs_3_, ...), custom_call_target="tpu_custom_call" | custom-call | bytes 10500000 | tf_op jit(solution)/shard_map/rise/pallas_call | solution.py:299
  92.1 3.5 %collective-permute-done.26.refs_3_ = bf16[128,1024]{1,0:T(8,128)(2,1)S(1)} collective-permute-done((bf16[128,1024]{1,0:T(8,128)(2,1)S(1)}, bf16[128,1024]{1,0:T(8,128)(2,1)S(1)}, u32[]{:S(2)}, u32[]{:S(2)}) %collective-permute-start.26) | collective-permute-done | bytes 262176 | tf_op jit(solution)/shard_map/ppermute | solution.py:418
  97.6 3.1 %rise.7.refs_0_ = bf16[256,1024]{1,0:T(8,128)(2,1)S(1)} custom-call(bf16[128,1024]{1,0:T(8,128)(2,1)S(1)} %collective-permute-done.19.refs_0_, bf16[128,1024]{1,0:T(8,128)(2,1)S(1)} %collective-permute-done.23.refs_1_, bf16[128,1024]{1,0:T(8,128)(2,1)S(1)} %collective-permute-done.25.refs_2_, bf16[128,1024]{1,0:T(8,128)(2,1)S(1)} %collective-permute-done.26.refs_3_, ...), custom_call_target="tpu_custom_call" | custom-call | bytes 10500000 | tf_op jit(solution)/shard_map/rise/pallas_call | solution.py:299
  101.9 2.6 %collective-permute-done.27.refs_2_ = bf16[128,1024]{1,0:T(8,128)(2,1)S(1)} collective-permute-done((bf16[128,1024]{1,0:T(8,128)(2,1)S(1)}, bf16[128,1024]{1,0:T(8,128)(2,1)S(1)}, u32[]{:S(2)}, u32[]{:S(2)}) %collective-permute-start.27) | collective-permute-done | bytes 262176 | tf_op jit(solution)/shard_map/ppermute | solution.py:418
  104.6 2.8 %collective-permute-done.28.refs_3_ = bf16[128,1024]{1,0:T(8,128)(2,1)S(1)} collective-permute-done((bf16[128,1024]{1,0:T(8,128)(2,1)S(1)}, bf16[128,1024]{1,0:T(8,128)(2,1)S(1)}, u32[]{:S(2)}, u32[]{:S(2)}) %collective-permute-start.28) | collective-permute-done | bytes 262176 | tf_op jit(solution)/shard_map/ppermute | solution.py:418
  123.7 3.1 %rise.6.refs_0_ = bf16[256,1024]{1,0:T(8,128)(2,1)S(1)} custom-call(bf16[128,1024]{1,0:T(8,128)(2,1)S(1)} %collective-permute-done.22.refs_0_, bf16[128,1024]{1,0:T(8,128)(2,1)S(1)} %collective-permute-done.24.refs_1_, bf16[128,1024]{1,0:T(8,128)(2,1)S(1)} %collective-permute-done.27.refs_2_, bf16[128,1024]{1,0:T(8,128)(2,1)S(1)} %collective-permute-done.28.refs_3_, ...), custom_call_target="tpu_custom_call" | custom-call | bytes 10500000 | tf_op jit(solution)/shard_map/rise/pallas_call | solution.py:299
  135.0 3.1 %rise.4.refs_0_ = bf16[256,1024]{1,0:T(8,128)(2,1)S(1)} custom-call(bf16[128,1024]{1,0:T(8,128)(2,1)S(1)} %get-tuple-element.83.refs_0_, bf16[128,1024]{1,0:T(8,128)(2,1)S(1)} %get-tuple-element.84.refs_1_, bf16[128,1024]{1,0:T(8,128)(2,1)S(1)} %collective-permute-done.13.refs_2_, bf16[128,1024]{1,0:T(8,128)(2,1)S(1)} %collective-permute-done.14.refs_3_, ...), custom_call_target="tpu_custom_call" | custom-call | bytes 10500000 | tf_op jit(solution)/shard_map/rise/pallas_call | solution.py:299
  146.9 3.3 %collective-permute-done.34.refs_1_ = bf16[128,1024]{1,0:T(8,128)(2,1)S(1)} collective-permute-done((bf16[128,1024]{1,0:T(8,128)(2,1)S(1)}, bf16[128,1024]{1,0:T(8,128)(2,1)S(1)}, u32[]{:S(2)}, u32[]{:S(2)}) %collective-permute-start.34) | collective-permute-done | bytes 262176 | tf_op jit(solution)/shard_map/ppermute | solution.py:519
  150.2 5.2 %collective-permute-done.43.refs_4_ = bf16[128,1024]{1,0:T(8,128)(2,1)S(1)} collective-permute-done((bf16[128,1024]{1,0:T(8,128)(2,1)S(1)}, bf16[128,1024]{1,0:T(8,128)(2,1)S(1)}, u32[]{:S(2)}, u32[]{:S(2)}) %collective-permute-start.43) | collective-permute-done | bytes 262176 | tf_op jit(solution)/shard_map/ppermute | solution.py:519
  (112 shorter events, 71.2 us)
Async XLA Ops:
  6.8 32.4 %collective-permute-start.8 = (bf16[512,1024]{1,0:T(8,128)(2,1)}, bf16[512,1024]{1,0:T(8,128)(2,1)S(1)}, u32[]{:S(2)}, u32[]{:S(2)}) collective-permute-start(bf16[512,1024]{1,0:T(8,128)(2,1)} %refs_4_.7), channel_id=1, source_target_pairs={{0,16},{8,24},{16,0},{24,8},{1,17},{9,25},{17,1},{25,9},{2,18},{10... | collective-permute-start | bytes 3145736 | tf_op jit(solution)/shard_map/ppermute | solution.py:423
  13.0 26.1 %collective-permute-start.7 = (bf16[512,1024]{1,0:T(8,128)(2,1)}, bf16[512,1024]{1,0:T(8,128)(2,1)S(1)}, u32[]{:S(2)}, u32[]{:S(2)}) collective-permute-start(bf16[512,1024]{1,0:T(8,128)(2,1)} %refs_4_.7), channel_id=1, source_target_pairs={{0,8},{8,0},{16,24},{24,16},{1,9},{9,1},{17,25},{25,17},{2,10},{10... | collective-permute-start | bytes 3145736 | tf_op jit(solution)/shard_map/ppermute | solution.py:427
  13.0 15.0 %collective-permute-start.4 = (bf16[2,256,256]{2,1,0:T(8,128)(2,1)S(1)}, bf16[2,256,256]{2,1,0:T(8,128)(2,1)S(1)}, u32[]{:S(2)}, u32[]{:S(2)}) collective-permute-start(bf16[2,256,256]{2,1,0:T(8,128)(2,1)S(1)} %collective-permute-done.2.refs_9_), channel_id=1, source_target_pairs={{0,4},{1,5},{4,6},{5,7},{6,2},{7,3},{2,0},{3,1},{8,12},{9,13},{12,... | collective-permute-start | bytes 786440 | tf_op jit(solution)/shard_map/ppermute | solution.py:415
  14.6 13.4 %collective-permute-start.3 = (bf16[2,256,256]{2,1,0:T(8,128)(2,1)S(1)}, bf16[2,256,256]{2,1,0:T(8,128)(2,1)S(1)}, u32[]{:S(2)}, u32[]{:S(2)}) collective-permute-start(bf16[2,256,256]{2,1,0:T(8,128)(2,1)S(1)} %collective-permute-done.2.refs_9_), channel_id=1, source_target_pairs={{0,1},{1,0},{4,5},{5,4},{6,7},{7,6},{2,3},{3,2},{8,9},{9,8},{12,13... | collective-permute-start | bytes 786440 | tf_op jit(solution)/shard_map/ppermute | solution.py:418
  31.2 12.9 %collective-permute-start.10 = (bf16[512,1024]{1,0:T(8,128)(2,1)}, bf16[512,1024]{1,0:T(8,128)(2,1)S(1)}, u32[]{:S(2)}, u32[]{:S(2)}) collective-permute-start(bf16[512,1024]{1,0:T(8,128)(2,1)} %refs_8_.7), channel_id=1, source_target_pairs={{0,8},{8,0},{16,24},{24,16},{1,9},{9,1},{17,25},{25,17},{2,10},{10... | collective-permute-start | bytes 3145736 | tf_op jit(solution)/shard_map/ppermute | solution.py:427
  39.7 25.1 %collective-permute-start.15 = (bf16[512,1024]{1,0:T(8,128)(2,1)S(1)}, bf16[512,1024]{1,0:T(8,128)(2,1)S(1)}, u32[]{:S(2)}, u32[]{:S(2)}) collective-permute-start(bf16[512,1024]{1,0:T(8,128)(2,1)S(1)} %copy-done.1), channel_id=1, source_target_pairs={{0,16},{8,24},{16,0},{24,8},{1,17},{9,25},{17,1},{25,9},{2,18},{10... | collective-permute-start | bytes 3145736 | tf_op jit(solution)/shard_map/ppermute | solution.py:423
  51.7 13.2 %collective-permute-start.16 = (bf16[128,1024]{1,0:T(8,128)(2,1)S(1)}, bf16[128,1024]{1,0:T(8,128)(2,1)S(1)}, u32[]{:S(2)}, u32[]{:S(2)}) collective-permute-start(bf16[128,1024]{1,0:T(8,128)(2,1)S(1)} %get-tuple-element.83.refs_0_), channel_id=1, source_target_pairs={{0,4},{1,5},{4,6},{5,7},{6,2},{7,3},{2,0},{3,1},{8,12},{9,13},{12,... | collective-permute-start | bytes 786440 | tf_op jit(solution)/shard_map/ppermute | solution.py:415
  52.9 11.9 %collective-permute-start.13 = (bf16[128,1024]{1,0:T(8,128)(2,1)S(1)}, bf16[128,1024]{1,0:T(8,128)(2,1)S(1)}, u32[]{:S(2)}, u32[]{:S(2)}) collective-permute-start(bf16[128,1024]{1,0:T(8,128)(2,1)S(1)} %get-tuple-element.83.refs_0_), channel_id=1, source_target_pairs={{0,1},{1,0},{4,5},{5,4},{6,7},{7,6},{2,3},{3,2},{8,9},{9,8},{12,13... | collective-permute-start | bytes 786440 | tf_op jit(solution)/shard_map/ppermute | solution.py:418
  53.2 11.7 %collective-permute-start.17 = (bf16[128,1024]{1,0:T(8,128)(2,1)S(1)}, bf16[128,1024]{1,0:T(8,128)(2,1)S(1)}, u32[]{:S(2)}, u32[]{:S(2)}) collective-permute-start(bf16[128,1024]{1,0:T(8,128)(2,1)S(1)} %get-tuple-element.84.refs_1_), channel_id=1, source_target_pairs={{0,4},{1,5},{4,6},{5,7},{6,2},{7,3},{2,0},{3,1},{8,12},{9,13},{12,... | collective-permute-start | bytes 786440 | tf_op jit(solution)/shard_map/ppermute | solution.py:415
  53.9 11.5 %collective-permute-start.14 = (bf16[128,1024]{1,0:T(8,128)(2,1)S(1)}, bf16[128,1024]{1,0:T(8,128)(2,1)S(1)}, u32[]{:S(2)}, u32[]{:S(2)}) collective-permute-start(bf16[128,1024]{1,0:T(8,128)(2,1)S(1)} %get-tuple-element.84.refs_1_), channel_id=1, source_target_pairs={{0,1},{1,0},{4,5},{5,4},{6,7},{7,6},{2,3},{3,2},{8,9},{9,8},{12,13... | collective-permute-start | bytes 786440 | tf_op jit(solution)/shard_map/ppermute | solution.py:418
  65.4 15.2 %collective-permute-start.18 = (bf16[512,1024]{1,0:T(8,128)(2,1)S(1)}, bf16[512,1024]{1,0:T(8,128)(2,1)S(1)}, u32[]{:S(2)}, u32[]{:S(2)}) collective-permute-start(bf16[512,1024]{1,0:T(8,128)(2,1)S(1)} %collective-permute-done.15.refs_10_), channel_id=1, source_target_pairs={{0,8},{8,0},{16,24},{24,16},{1,9},{9,1},{17,25},{25,17},{2,10},{10... | collective-permute-start | bytes 3145736 | tf_op jit(solution)/shard_map/ppermute | solution.py:427
  67.2 13.5 %collective-permute-start.21 = (bf16[128,1024]{1,0:T(8,128)(2,1)S(1)}, bf16[128,1024]{1,0:T(8,128)(2,1)S(1)}, u32[]{:S(2)}, u32[]{:S(2)}) collective-permute-start(bf16[128,1024]{1,0:T(8,128)(2,1)S(1)} %collective-permute-done.17.refs_1_), channel_id=1, source_target_pairs={{0,1},{1,0},{4,5},{5,4},{6,7},{7,6},{2,3},{3,2},{8,9},{9,8},{12,13... | collective-permute-start | bytes 786440 | tf_op jit(solution)/shard_map/ppermute | solution.py:418
  68.6 12.0 %collective-permute-start.23 = (bf16[128,1024]{1,0:T(8,128)(2,1)S(1)}, bf16[128,1024]{1,0:T(8,128)(2,1)S(1)}, u32[]{:S(2)}, u32[]{:S(2)}) collective-permute-start(bf16[128,1024]{1,0:T(8,128)(2,1)S(1)} %collective-permute-done.17.refs_1_), channel_id=1, source_target_pairs={{0,4},{1,5},{4,6},{5,7},{6,2},{7,3},{2,0},{3,1},{8,12},{9,13},{12,... | collective-permute-start | bytes 786440 | tf_op jit(solution)/shard_map/ppermute | solution.py:415
  80.6 26.7 %collective-permute-start.36 = (bf16[1024,512]{1,0:T(8,128)(2,1)S(1)}, bf16[1024,512]{1,0:T(8,128)(2,1)S(1)}, u32[]{:S(2)}, u32[]{:S(2)}) collective-permute-start(bf16[1024,512]{1,0:T(8,128)(2,1)S(1)} %copy-done.2), channel_id=1, source_target_pairs={{0,16},{8,24},{16,0},{24,8},{1,17},{9,25},{17,1},{25,9},{2,18},{10... | collective-permute-start | bytes 3145736 | tf_op jit(solution)/shard_map/ppermute | solution.py:423
  83.0 12.6 %collective-permute-start.26 = (bf16[128,1024]{1,0:T(8,128)(2,1)S(1)}, bf16[128,1024]{1,0:T(8,128)(2,1)S(1)}, u32[]{:S(2)}, u32[]{:S(2)}) collective-permute-start(bf16[128,1024]{1,0:T(8,128)(2,1)S(1)} %collective-permute-done.23.refs_1_), channel_id=1, source_target_pairs={{0,1},{1,0},{4,5},{5,4},{6,7},{7,6},{2,3},{3,2},{8,9},{9,8},{12,13... | collective-permute-start | bytes 786440 | tf_op jit(solution)/shard_map/ppermute | solution.py:418
  96.0 11.4 %collective-permute-start.28 = (bf16[128,1024]{1,0:T(8,128)(2,1)S(1)}, bf16[128,1024]{1,0:T(8,128)(2,1)S(1)}, u32[]{:S(2)}, u32[]{:S(2)}) collective-permute-start(bf16[128,1024]{1,0:T(8,128)(2,1)S(1)} %collective-permute-done.24.refs_1_), channel_id=1, source_target_pairs={{0,1},{1,0},{4,5},{5,4},{6,7},{7,6},{2,3},{3,2},{8,9},{9,8},{12,13... | collective-permute-start | bytes 786440 | tf_op jit(solution)/shard_map/ppermute | solution.py:418
  111.3 10.8 %collective-permute-start.40 = (bf16[128,1024]{1,0:T(8,128)(2,1)S(1)}, bf16[128,1024]{1,0:T(8,128)(2,1)S(1)}, u32[]{:S(2)}, u32[]{:S(2)}) collective-permute-start(bf16[128,1024]{1,0:T(8,128)(2,1)S(1)} %get-tuple-element.115), channel_id=1, source_target_pairs={{0,1},{1,0},{4,5},{5,4},{6,7},{7,6},{2,3},{3,2},{8,9},{9,8},{12,13... | collective-permute-start | bytes 786440 | tf_op jit(solution)/shard_map/ppermute | solution.py:519
  113.2 15.5 %collective-permute-start.30 = (bf16[128,1024]{1,0:T(8,128)(2,1)S(1)}, bf16[128,1024]{1,0:T(8,128)(2,1)S(1)}, u32[]{:S(2)}, u32[]{:S(2)}) collective-permute-start(bf16[128,1024]{1,0:T(8,128)(2,1)S(1)} %get-tuple-element.102), channel_id=1, source_target_pairs={{0,1},{1,0},{4,5},{5,4},{6,7},{7,6},{2,3},{3,2},{8,9},{9,8},{12,13... | collective-permute-start | bytes 786440 | tf_op jit(solution)/shard_map/ppermute | solution.py:519
  116.6 12.2 %collective-permute-start.32 = (bf16[128,1024]{1,0:T(8,128)(2,1)S(1)}, bf16[128,1024]{1,0:T(8,128)(2,1)S(1)}, u32[]{:S(2)}, u32[]{:S(2)}) collective-permute-start(bf16[128,1024]{1,0:T(8,128)(2,1)S(1)} %add_convert_fusion.5), channel_id=1, source_target_pairs={{0,4},{1,5},{4,6},{5,7},{6,2},{7,3},{2,0},{3,1},{8,12},{9,13},{12,... | collective-permute-start | bytes 786440 | tf_op jit(solution)/shard_map/ppermute | solution.py:415
  119.3 14.0 %collective-permute-start.39 = (bf16[128,1024]{1,0:T(8,128)(2,1)S(1)}, bf16[128,1024]{1,0:T(8,128)(2,1)S(1)}, u32[]{:S(2)}, u32[]{:S(2)}) collective-permute-start(bf16[128,1024]{1,0:T(8,128)(2,1)S(1)} %get-tuple-element.113), channel_id=1, source_target_pairs={{0,1},{1,0},{4,5},{5,4},{6,7},{7,6},{2,3},{3,2},{8,9},{9,8},{12,13... | collective-permute-start | bytes 786440 | tf_op jit(solution)/shard_map/ppermute | solution.py:519
  122.2 11.2 %collective-permute-start.41 = (bf16[128,1024]{1,0:T(8,128)(2,1)S(1)}, bf16[128,1024]{1,0:T(8,128)(2,1)S(1)}, u32[]{:S(2)}, u32[]{:S(2)}) collective-permute-start(bf16[128,1024]{1,0:T(8,128)(2,1)S(1)} %add_convert_fusion.2), channel_id=1, source_target_pairs={{0,4},{1,5},{4,6},{5,7},{6,2},{7,3},{2,0},{3,1},{8,12},{9,13},{12,... | collective-permute-start | bytes 786440 | tf_op jit(solution)/shard_map/ppermute | solution.py:415
  128.0 11.3 %collective-permute-start.29 = (bf16[128,1024]{1,0:T(8,128)(2,1)S(1)}, bf16[128,1024]{1,0:T(8,128)(2,1)S(1)}, u32[]{:S(2)}, u32[]{:S(2)}) collective-permute-start(bf16[128,1024]{1,0:T(8,128)(2,1)S(1)} %get-tuple-element.100), channel_id=1, source_target_pairs={{0,1},{1,0},{4,5},{5,4},{6,7},{7,6},{2,3},{3,2},{8,9},{9,8},{12,13... | collective-permute-start | bytes 786440 | tf_op jit(solution)/shard_map/ppermute | solution.py:519
  130.6 14.0 %collective-permute-start.38 = (bf16[128,1024]{1,0:T(8,128)(2,1)S(1)}, bf16[128,1024]{1,0:T(8,128)(2,1)S(1)}, u32[]{:S(2)}, u32[]{:S(2)}) collective-permute-start(bf16[128,1024]{1,0:T(8,128)(2,1)S(1)} %get-tuple-element.111), channel_id=1, source_target_pairs={{0,1},{1,0},{4,5},{5,4},{6,7},{7,6},{2,3},{3,2},{8,9},{9,8},{12,13... | collective-permute-start | bytes 786440 | tf_op jit(solution)/shard_map/ppermute | solution.py:519
  133.5 11.1 %collective-permute-start.42 = (bf16[128,1024]{1,0:T(8,128)(2,1)S(1)}, bf16[128,1024]{1,0:T(8,128)(2,1)S(1)}, u32[]{:S(2)}, u32[]{:S(2)}) collective-permute-start(bf16[128,1024]{1,0:T(8,128)(2,1)S(1)} %add_convert_fusion.1), channel_id=1, source_target_pairs={{0,4},{1,5},{4,6},{5,7},{6,2},{7,3},{2,0},{3,1},{8,12},{9,13},{12,... | collective-permute-start | bytes 786440 | tf_op jit(solution)/shard_map/ppermute | solution.py:415
  (31 other events, 395.8 us)

commit v2 on v1

--- a/solution.py
+++ b/solution.py
@@ -191,7 +191,7 @@
         out_shape=[shape] * 3,
         in_specs=[vmem] * len(operands),
         out_specs=[vmem] * 3,
-        compiler_params=pltpu.CompilerParams(vmem_limit_bytes=20 * 2**20),
+        compiler_params=pltpu.CompilerParams(vmem_limit_bytes=(8 + 3 * len(blocks)) * 2**20),
         cost_estimate=cost(1.1 * len(blocks)),
         name="attend",
     )(*operands)
@@ -449,18 +449,18 @@
     ready, state = [], None
     for zs in range(1, depth_z):
         if zs == depth_z - 1:
-            ready += [gate_swap, *gate_rows[1:]]
+            state = attend(q, None, blocks)
+            blocks, ready = [], [state[0], gate_swap, *gate_rows[1:]]
         here = tie(arriving, *other, *ready)
         if zs < depth_z - 1:
-            arriving = round_z(here)
+            arriving, ready = round_z(here), [q, before]
         blocks += [(b, prefix_mask) for b in other + [here]]
         other = along_y(here)
-        state = attend(q, state, blocks)
-        blocks, ready = [], [state[0]]
         if zs == 1:
             gate_swap = other_core(w_gate, here)
         elif zs == 2:
             up_swap = other_core(w_up, here)
+    state = attend(q, state, blocks)
     down_swap = other_core(w_down, here)
     up_rows = along_x(w_up, *gate_rows[1:], here)
     gates = [w_gate, gate_swap]
@@ -479,21 +479,14 @@
     arrived, across = [normed], [[along_y(half) for half in normed]]
     ups, downs, acts = [w_up, up_swap], [w_down, down_swap], {}
     for zs in range(1, depth_z):
-        before = [b for c in across[zs - 2] for b in c] if zs > 1 else []
-        waits = [before for _ in normed]
-        if zs == depth_z - 1:
-            down_cols = along_x(w_down, *ups[3:], *arrived[2], *[b for c in across[1] for b in c])
-        if zs == depth_z - 1:
-            acts[1] = rise([arrived[1]] + [list(c) for c in zip(*across[1])], gates, ups)
-            acts[0] = rise([arrived[0]] + [list(c) for c in zip(*across[0])], gates, ups)
+        waits = across[zs - 2] if zs > 1 else [[] for _ in normed]
         arrived.append([round_z(half, *wait) for half, wait in zip(arrived[-1], waits)])
-        if zs == 1:
+        across.append([along_y(half, *arrived[zs][1:]) for half in arrived[zs]])
+        if zs == depth_z - 2:
             for up in up_rows[1:]:
-                ups += [up, other_core(up, *arrived[1], *[b for c in across[0] for b in c])]
-        late = arrived[zs][1:] + [b for c in across[-1] for b in c]
-        if zs == depth_z - 1:
-            late += [acts[1]]
-        across.append([along_y(half, *late) for half in arrived[zs]])
+                ups += [up, other_core(up, *arrived[zs], *across[zs - 1][0])]
+            down_cols = along_x(w_down, *up_rows[1:], *arrived[zs], *[b for c in across[zs - 1] for b in c])
+    acts[1] = rise([arrived[1]] + [list(c) for c in zip(*across[1])], gates, ups)
     chunks = [[a] + [list(c) for c in zip(*b)] for a, b in zip(arrived, across)]
     each = grps // HALVES
     fallen = {}

time: 157 us -> 150 us (0.955)
  waiting for transfers between devices: 66.9 us -> 57.3 us
  starting transfers between devices: 48 us -> 52.7 us
  Pallas kernels: 35.5 us -> 33.9 us
    ppermute x15, waiting for transfers between devices: 13 us -> 25.9 us  [round_z(): return lax.ppermute(tie(block, *others), 'dev', shift(1, 0))]
    ppermute x3, waiting for transfers between devices: 9.33 us -> 0.01 us  [along_x(): blocks.append(lax.ppermute(tie(blocks[-1], *others), 'grp', x_shift))]
    ppermute x12, waiting for transfers between devices: 26.3 us -> 17.7 us  [along_y(): lax.ppermute(tie(block, *others), 'dev', shift(0, ys))]
    ppermute x15, starting transfers between devices: 22.2 us -> 28.1 us  [round_z(): return lax.ppermute(tie(block, *others), 'dev', shift(1, 0))]
    ppermute x8, waiting for transfers between devices: 15.6 us -> 10.6 us  [shards(): lax.ppermute(parts[ys], 'dev', shift(0, -ys))]
    pallas_call x3 -> x2, Pallas kernels: 8.33 us -> 6.83 us  [attend(): pl.pallas_call(kernel, out_shape=[shape] * 3, in_specs=[vmem] * len(opera...]
  transfers between devices with their start and end apart: 45 -> 45, of which waited for: 23 -> 24; matrix products, arithmetic and copies ran while one was open for 1% -> 1% of each run, Pallas kernels for 22% -> 22%
where the time goes in v2:
time: 150 us
  waiting for transfers between devices  57.3 us (38%)
  starting transfers between devices  52.7 us (35%)
  Pallas kernels  33.9 us (23%)
  local copies, waits for them, and re-layouts  2.94 us (2%)
  other arithmetic  2.65 us (2%)
    ppermute x15, starting transfers between devices, round_z(): return lax.ppermute(tie(block, *others), 'dev', shift(1, 0))  28.1 us
    ppermute x15, waiting for transfers between devices, round_z(): return lax.ppermute(tie(block, *others), 'dev', shift(1, 0))  25.9 us
    ppermute x12, waiting for transfers between devices, along_y(): lax.ppermute(tie(block, *others), 'dev', shift(0, ys))  17.7 us
    pallas_call x4, Pallas kernels, rise(): pl.pallas_call(kernel, out_shape=jax.ShapeDtypeStruct((parts * tokens, hi...  12.3 us
    ppermute x12, starting transfers between devices, along_y(): lax.ppermute(tie(block, *others), 'dev', shift(0, ys))  10.8 us
    ppermute x8, waiting for transfers between devices, shards(): lax.ppermute(parts[ys], 'dev', shift(0, -ys))  10.6 us
    pallas_call x8, Pallas kernels, fall(): pl.pallas_call(kernel, out_shape=[shape] * parts, in_specs=[vmem] * (1 +...  9.8 us
    ppermute x8, starting transfers between devices, shards(): lax.ppermute(parts[ys], 'dev', shift(0, -ys))  7.37 us
  transfers between devices with their start and end apart: 45, of which 24 were waited for; matrix products, arithmetic and copies ran while one was open for 1% of the time, Pallas kernels for 22%

profile of v2, /device:TPU:0, one launch (start us, length us, event | category | flops | bytes accessed | tf_op | source)
XLA Modules:
  0.0 149.9 jit_solution(5330529257424624392)
XLA Ops:
  1.2 4.1 %collective-permute-start.2 = (bf16[2,256,256]{2,1,0:T(8,128)(2,1)S(1)}, bf16[2,256,256]{2,1,0:T(8,128)(2,1)S(1)}, u32[]{:S(2)}, u32[]{:S(2)}) collective-permute-start(bf16[2,256,256]{2,1,0:T(8,128)(2,1)S(1)} %pad_maximum_fusion.refs_5_), channel_id=1, source_target_pairs={{0,4},{1,5},{4,6},{5,7},{6,2},{7,3},{2,0},{3,1},{8,12},{9,13},{12,... | collective-permute-start | bytes 786440 | tf_op jit(solution)/shard_map/ppermute | solution.py:415
  8.3 2.6 %collective-permute-done.2.refs_9_ = bf16[2,256,256]{2,1,0:T(8,128)(2,1)S(1)} collective-permute-done((bf16[2,256,256]{2,1,0:T(8,128)(2,1)S(1)}, bf16[2,256,256]{2,1,0:T(8,128)(2,1)S(1)}, u32[]{:S(2)}, u32[]{:S(2)}) %collective-permute-start.2) | collective-permute-done | bytes 262176 | tf_op jit(solution)/shard_map/ppermute | solution.py:415
  17.0 2.4 %collective-permute-start = (bf16[2,128,256]{2,1,0:T(8,128)(2,1)S(1)}, bf16[2,128,256]{2,1,0:T(8,128)(2,1)S(1)}, u32[]{:S(2)}, u32[]{:S(2)}) collective-permute-start(bf16[2,128,256]{2,1,0:T(8,128)(2,1)S(1)} %pad_maximum_fusion.1.refs_3_), channel_id=1, source_target_pairs={{0,1},{1,2},{2,3},{3,4},{4,5},{5,6},{6,7},{8,9},{9,10},{10,11},{11... | collective-permute-start | bytes 393224 | tf_op jit(solution)/shard_map/ppermute | solution.py:437
  24.9 3.1 %collective-permute-start.6 = (bf16[2,256,256]{2,1,0:T(8,128)(2,1)S(1)}, bf16[2,256,256]{2,1,0:T(8,128)(2,1)S(1)}, u32[]{:S(2)}, u32[]{:S(2)}) collective-permute-start(bf16[2,256,256]{2,1,0:T(8,128)(2,1)S(1)} %collective-permute-done.4.refs_13_), channel_id=1, source_target_pairs={{0,4},{1,5},{4,6},{5,7},{6,2},{7,3},{2,0},{3,1},{8,12},{9,13},{12,... | collective-permute-start | bytes 786440 | tf_op jit(solution)/shard_map/ppermute | solution.py:415
  28.0 4.3 %attend.2 = (f32[2,512,128]{2,1,0:T(8,128)S(1)}, f32[2,512,128]{2,1,0:T(8,128)S(1)}, f32[2,512,128]{2,1,0:T(8,128)S(1)}) custom-call(bf16[2,1024,128]{2,1,0:T(8,128)(2,1)S(1)} %get-tuple-element.58.refs_0_, bf16[2,128,256]{2,1,0:T(8,128)(2,1)S(1)} %collective-permute-done.refs_1_, f32[128,128]{1,0:T(8,128)S(1)} %get-tuple-element.59.refs_2_, ...), custom_call_target="tpu_custom_call" | custom-call | bytes 26950000 | tf_op jit(solution)/shard_map/attend/pallas_call | solution.py:189
  33.7 2.2 %collective-permute-done.5.refs_4_ = bf16[2,256,256]{2,1,0:T(8,128)(2,1)S(1)} collective-permute-done((bf16[2,256,256]{2,1,0:T(8,128)(2,1)S(1)}, bf16[2,256,256]{2,1,0:T(8,128)(2,1)S(1)}, u32[]{:S(2)}, u32[]{:S(2)}) %collective-permute-start.5) | collective-permute-done | bytes 262176 | tf_op jit(solution)/shard_map/ppermute | solution.py:418
  38.2 2.5 %attend.3 = (f32[2,512,128]{2,1,0:T(8,128)S(1)}, f32[2,512,128]{2,1,0:T(8,128)S(1)}, f32[2,512,128]{2,1,0:T(8,128)S(1)}) custom-call(bf16[2,1024,128]{2,1,0:T(8,128)(2,1)S(1)} %get-tuple-element.58.refs_0_, f32[2,512,128]{2,1,0:T(8,128)S(1)} %get-tuple-element.64.refs_1_, f32[2,512,128]{2,1,0:T(8,128)S(1)} %get-tuple-element.65.refs_2_, ...), custom_call_target="tpu_custom_call" | custom-call | bytes 7700000 | tf_op jit(solution)/shard_map/attend/pallas_call | solution.py:189
  40.8 5.1 %collective-permute-done.9.refs_4_ = bf16[2,256,256]{2,1,0:T(8,128)(2,1)S(1)} collective-permute-done((bf16[2,256,256]{2,1,0:T(8,128)(2,1)S(1)}, bf16[2,256,256]{2,1,0:T(8,128)(2,1)S(1)}, u32[]{:S(2)}, u32[]{:S(2)}) %collective-permute-start.9) | collective-permute-done | bytes 262176 | tf_op jit(solution)/shard_map/ppermute | solution.py:418
  46.0 2.4 %attend_project.1 = (f32[128,2048]{1,0:T(8,128)S(1)}, bf16[128,1024]{1,0:T(8,128)(2,1)S(1)}, bf16[128,1024]{1,0:T(8,128)(2,1)S(1)}) custom-call(bf16[2,1024,128]{2,1,0:T(8,128)(2,1)S(1)} %get-tuple-element.58.refs_0_, f32[2,512,128]{2,1,0:T(8,128)S(1)} %get-tuple-element.69.refs_1_, f32[2,512,128]{2,1,0:T(8,128)S(1)} %get-tuple-element.70.refs_2_, ...), custom_call_target="tpu_custom_call" | custom-call | bytes 10850000 | tf_op jit(solution)/shard_map/attend_project/pallas_call | solution.py:252
  52.2 5.4 %collective-permute-done.16.refs_0_ = bf16[128,1024]{1,0:T(8,128)(2,1)S(1)} collective-permute-done((bf16[128,1024]{1,0:T(8,128)(2,1)S(1)}, bf16[128,1024]{1,0:T(8,128)(2,1)S(1)}, u32[]{:S(2)}, u32[]{:S(2)}) %collective-permute-start.16) | collective-permute-done | bytes 262176 | tf_op jit(solution)/shard_map/ppermute | solution.py:415
  59.8 3.5 %collective-permute-done.18.refs_1_ = bf16[128,1024]{1,0:T(8,128)(2,1)S(1)} collective-permute-done((bf16[128,1024]{1,0:T(8,128)(2,1)S(1)}, bf16[128,1024]{1,0:T(8,128)(2,1)S(1)}, u32[]{:S(2)}, u32[]{:S(2)}) %collective-permute-start.18) | collective-permute-done | bytes 262176 | tf_op jit(solution)/shard_map/ppermute | solution.py:415
  76.6 6.5 %collective-permute-done.24.refs_1_ = bf16[128,1024]{1,0:T(8,128)(2,1)S(1)} collective-permute-done((bf16[128,1024]{1,0:T(8,128)(2,1)S(1)}, bf16[128,1024]{1,0:T(8,128)(2,1)S(1)}, u32[]{:S(2)}, u32[]{:S(2)}) %collective-permute-start.24) | collective-permute-done | bytes 262176 | tf_op jit(solution)/shard_map/ppermute | solution.py:415
  83.8 3.2 %collective-permute-done.22.refs_0_ = bf16[128,1024]{1,0:T(8,128)(2,1)S(1)} collective-permute-done((bf16[128,1024]{1,0:T(8,128)(2,1)S(1)}, bf16[128,1024]{1,0:T(8,128)(2,1)S(1)}, u32[]{:S(2)}, u32[]{:S(2)}) %collective-permute-start.22) | collective-permute-done | bytes 262176 | tf_op jit(solution)/shard_map/ppermute | solution.py:415
  89.0 3.1 %rise.7.refs_0_ = bf16[256,1024]{1,0:T(8,128)(2,1)S(1)} custom-call(bf16[128,1024]{1,0:T(8,128)(2,1)S(1)} %collective-permute-done.16.refs_0_, bf16[128,1024]{1,0:T(8,128)(2,1)S(1)} %collective-permute-done.18.refs_1_, bf16[128,1024]{1,0:T(8,128)(2,1)S(1)} %collective-permute-done.20.refs_2_, bf16[128,1024]{1,0:T(8,128)(2,1)S(1)} %collective-permute-done.23.refs_3_, ...), custom_call_target="tpu_custom_call" | custom-call | bytes 10500000 | tf_op jit(solution)/shard_map/rise/pallas_call | solution.py:299
  93.4 3.1 %rise.6.refs_0_ = bf16[256,1024]{1,0:T(8,128)(2,1)S(1)} custom-call(bf16[128,1024]{1,0:T(8,128)(2,1)S(1)} %collective-permute-done.17.refs_0_, bf16[128,1024]{1,0:T(8,128)(2,1)S(1)} %collective-permute-done.19.refs_1_, bf16[128,1024]{1,0:T(8,128)(2,1)S(1)} %collective-permute-done.28.refs_2_, bf16[128,1024]{1,0:T(8,128)(2,1)S(1)} %collective-permute-done.29.refs_3_, ...), custom_call_target="tpu_custom_call" | custom-call | bytes 10500000 | tf_op jit(solution)/shard_map/rise/pallas_call | solution.py:299
  96.6 4.1 %collective-permute-done.26.refs_3_ = bf16[128,1024]{1,0:T(8,128)(2,1)S(1)} collective-permute-done((bf16[128,1024]{1,0:T(8,128)(2,1)S(1)}, bf16[128,1024]{1,0:T(8,128)(2,1)S(1)}, u32[]{:S(2)}, u32[]{:S(2)}) %collective-permute-start.26) | collective-permute-done | bytes 262176 | tf_op jit(solution)/shard_map/ppermute | solution.py:418
  109.9 2.7 %collective-permute-start.32 = (bf16[128,1024]{1,0:T(8,128)(2,1)S(1)}, bf16[128,1024]{1,0:T(8,128)(2,1)S(1)}, u32[]{:S(2)}, u32[]{:S(2)}) collective-permute-start(bf16[128,1024]{1,0:T(8,128)(2,1)S(1)} %add_convert_fusion.5), channel_id=1, source_target_pairs={{0,4},{1,5},{4,6},{5,7},{6,2},{7,3},{2,0},{3,1},{8,12},{9,13},{12,... | collective-permute-start | bytes 786440 | tf_op jit(solution)/shard_map/ppermute | solution.py:415
  115.6 2.7 %collective-permute-start.41 = (bf16[128,1024]{1,0:T(8,128)(2,1)S(1)}, bf16[128,1024]{1,0:T(8,128)(2,1)S(1)}, u32[]{:S(2)}, u32[]{:S(2)}) collective-permute-start(bf16[128,1024]{1,0:T(8,128)(2,1)S(1)} %add_convert_fusion.2), channel_id=1, source_target_pairs={{0,4},{1,5},{4,6},{5,7},{6,2},{7,3},{2,0},{3,1},{8,12},{9,13},{12,... | collective-permute-start | bytes 786440 | tf_op jit(solution)/shard_map/ppermute | solution.py:415
  118.3 3.1 %rise.5.refs_0_ = bf16[256,1024]{1,0:T(8,128)(2,1)S(1)} custom-call(bf16[128,1024]{1,0:T(8,128)(2,1)S(1)} %collective-permute-done.22.refs_0_, bf16[128,1024]{1,0:T(8,128)(2,1)S(1)} %collective-permute-done.24.refs_1_, bf16[128,1024]{1,0:T(8,128)(2,1)S(1)} %collective-permute-done.25.refs_2_, bf16[128,1024]{1,0:T(8,128)(2,1)S(1)} %collective-permute-done.26.refs_3_, ...), custom_call_target="tpu_custom_call" | custom-call | bytes 10500000 | tf_op jit(solution)/shard_map/rise/pallas_call | solution.py:299
  126.9 2.7 %collective-permute-start.42 = (bf16[128,1024]{1,0:T(8,128)(2,1)S(1)}, bf16[128,1024]{1,0:T(8,128)(2,1)S(1)}, u32[]{:S(2)}, u32[]{:S(2)}) collective-permute-start(bf16[128,1024]{1,0:T(8,128)(2,1)S(1)} %add_convert_fusion.1), channel_id=1, source_target_pairs={{0,4},{1,5},{4,6},{5,7},{6,2},{7,3},{2,0},{3,1},{8,12},{9,13},{12,... | collective-permute-start | bytes 786440 | tf_op jit(solution)/shard_map/ppermute | solution.py:415
  129.6 3.1 %rise.4.refs_0_ = bf16[256,1024]{1,0:T(8,128)(2,1)S(1)} custom-call(bf16[128,1024]{1,0:T(8,128)(2,1)S(1)} %get-tuple-element.77.refs_0_, bf16[128,1024]{1,0:T(8,128)(2,1)S(1)} %get-tuple-element.78.refs_1_, bf16[128,1024]{1,0:T(8,128)(2,1)S(1)} %collective-permute-done.13.refs_2_, bf16[128,1024]{1,0:T(8,128)(2,1)S(1)} %collective-permute-done.14.refs_3_, ...), custom_call_target="tpu_custom_call" | custom-call | bytes 10500000 | tf_op jit(solution)/shard_map/rise/pallas_call | solution.py:299
  138.8 3.0 %collective-permute-start.44 = (bf16[128,1024]{1,0:T(8,128)(2,1)S(1)}, bf16[128,1024]{1,0:T(8,128)(2,1)S(1)}, u32[]{:S(2)}, u32[]{:S(2)}) collective-permute-start(bf16[128,1024]{1,0:T(8,128)(2,1)S(1)} %add_convert_fusion), channel_id=1, source_target_pairs={{0,4},{1,5},{4,6},{5,7},{6,2},{7,3},{2,0},{3,1},{8,12},{9,13},{12,... | collective-permute-start | bytes 786440 | tf_op jit(solution)/shard_map/ppermute | solution.py:415
  141.8 2.7 %collective-permute-done.34.refs_1_ = bf16[128,1024]{1,0:T(8,128)(2,1)S(1)} collective-permute-done((bf16[128,1024]{1,0:T(8,128)(2,1)S(1)}, bf16[128,1024]{1,0:T(8,128)(2,1)S(1)}, u32[]{:S(2)}, u32[]{:S(2)}) %collective-permute-start.34) | collective-permute-done | bytes 262176 | tf_op jit(solution)/shard_map/ppermute | solution.py:512
  144.4 4.4 %collective-permute-done.43.refs_4_ = bf16[128,1024]{1,0:T(8,128)(2,1)S(1)} collective-permute-done((bf16[128,1024]{1,0:T(8,128)(2,1)S(1)}, bf16[128,1024]{1,0:T(8,128)(2,1)S(1)}, u32[]{:S(2)}, u32[]{:S(2)}) %collective-permute-start.43) | collective-permute-done | bytes 262176 | tf_op jit(solution)/shard_map/ppermute | solution.py:512
  (111 shorter events, 67.6 us)
Async XLA Ops:
  6.8 29.2 %collective-permute-start.8 = (bf16[512,1024]{1,0:T(8,128)(2,1)}, bf16[512,1024]{1,0:T(8,128)(2,1)S(1)}, u32[]{:S(2)}, u32[]{:S(2)}) collective-permute-start(bf16[512,1024]{1,0:T(8,128)(2,1)} %refs_4_.7), channel_id=1, source_target_pairs={{0,16},{8,24},{16,0},{24,8},{1,17},{9,25},{17,1},{25,9},{2,18},{10... | collective-permute-start | bytes 3145736 | tf_op jit(solution)/shard_map/ppermute | solution.py:423
  13.0 22.9 %collective-permute-start.7 = (bf16[512,1024]{1,0:T(8,128)(2,1)}, bf16[512,1024]{1,0:T(8,128)(2,1)S(1)}, u32[]{:S(2)}, u32[]{:S(2)}) collective-permute-start(bf16[512,1024]{1,0:T(8,128)(2,1)} %refs_4_.7), channel_id=1, source_target_pairs={{0,8},{8,0},{16,24},{24,16},{1,9},{9,1},{17,25},{25,17},{2,10},{10... | collective-permute-start | bytes 3145736 | tf_op jit(solution)/shard_map/ppermute | solution.py:427
  13.0 11.9 %collective-permute-start.4 = (bf16[2,256,256]{2,1,0:T(8,128)(2,1)S(1)}, bf16[2,256,256]{2,1,0:T(8,128)(2,1)S(1)}, u32[]{:S(2)}, u32[]{:S(2)}) collective-permute-start(bf16[2,256,256]{2,1,0:T(8,128)(2,1)S(1)} %collective-permute-done.2.refs_9_), channel_id=1, source_target_pairs={{0,4},{1,5},{4,6},{5,7},{6,2},{7,3},{2,0},{3,1},{8,12},{9,13},{12,... | collective-permute-start | bytes 786440 | tf_op jit(solution)/shard_map/ppermute | solution.py:415
  14.6 10.3 %collective-permute-start.3 = (bf16[2,256,256]{2,1,0:T(8,128)(2,1)S(1)}, bf16[2,256,256]{2,1,0:T(8,128)(2,1)S(1)}, u32[]{:S(2)}, u32[]{:S(2)}) collective-permute-start(bf16[2,256,256]{2,1,0:T(8,128)(2,1)S(1)} %collective-permute-done.2.refs_9_), channel_id=1, source_target_pairs={{0,1},{1,0},{4,5},{5,4},{6,7},{7,6},{2,3},{3,2},{8,9},{9,8},{12,13... | collective-permute-start | bytes 786440 | tf_op jit(solution)/shard_map/ppermute | solution.py:418
  28.0 12.8 %collective-permute-start.10 = (bf16[512,1024]{1,0:T(8,128)(2,1)}, bf16[512,1024]{1,0:T(8,128)(2,1)S(1)}, u32[]{:S(2)}, u32[]{:S(2)}) collective-permute-start(bf16[512,1024]{1,0:T(8,128)(2,1)} %refs_8_.7), channel_id=1, source_target_pairs={{0,8},{8,0},{16,24},{24,16},{1,9},{9,1},{17,25},{25,17},{2,10},{10... | collective-permute-start | bytes 3145736 | tf_op jit(solution)/shard_map/ppermute | solution.py:427
  36.4 31.0 %collective-permute-start.15 = (bf16[512,1024]{1,0:T(8,128)(2,1)}, bf16[512,1024]{1,0:T(8,128)(2,1)S(1)}, u32[]{:S(2)}, u32[]{:S(2)}) collective-permute-start(bf16[512,1024]{1,0:T(8,128)(2,1)} %refs_8_.7), channel_id=1, source_target_pairs={{0,16},{8,24},{16,0},{24,8},{1,17},{9,25},{17,1},{25,9},{2,18},{10... | collective-permute-start | bytes 3145736 | tf_op jit(solution)/shard_map/ppermute | solution.py:423
  49.9 13.3 %collective-permute-start.18 = (bf16[128,1024]{1,0:T(8,128)(2,1)S(1)}, bf16[128,1024]{1,0:T(8,128)(2,1)S(1)}, u32[]{:S(2)}, u32[]{:S(2)}) collective-permute-start(bf16[128,1024]{1,0:T(8,128)(2,1)S(1)} %get-tuple-element.78.refs_1_), channel_id=1, source_target_pairs={{0,4},{1,5},{4,6},{5,7},{6,2},{7,3},{2,0},{3,1},{8,12},{9,13},{12,... | collective-permute-start | bytes 786440 | tf_op jit(solution)/shard_map/ppermute | solution.py:415
  50.6 13.0 %collective-permute-start.14 = (bf16[128,1024]{1,0:T(8,128)(2,1)S(1)}, bf16[128,1024]{1,0:T(8,128)(2,1)S(1)}, u32[]{:S(2)}, u32[]{:S(2)}) collective-permute-start(bf16[128,1024]{1,0:T(8,128)(2,1)S(1)} %get-tuple-element.78.refs_1_), channel_id=1, source_target_pairs={{0,1},{1,0},{4,5},{5,4},{6,7},{7,6},{2,3},{3,2},{8,9},{9,8},{12,13... | collective-permute-start | bytes 786440 | tf_op jit(solution)/shard_map/ppermute | solution.py:418
  72.4 14.9 %collective-permute-start.21 = (bf16[512,1024]{1,0:T(8,128)(2,1)S(1)}, bf16[512,1024]{1,0:T(8,128)(2,1)S(1)}, u32[]{:S(2)}, u32[]{:S(2)}) collective-permute-start(bf16[512,1024]{1,0:T(8,128)(2,1)S(1)} %collective-permute-done.15.refs_10_), channel_id=1, source_target_pairs={{0,8},{8,0},{16,24},{24,16},{1,9},{9,1},{17,25},{25,17},{2,10},{10... | collective-permute-start | bytes 3145736 | tf_op jit(solution)/shard_map/ppermute | solution.py:427
  73.4 27.4 %collective-permute-start.36 = (bf16[1024,512]{1,0:T(8,128)(2,1)S(1)}, bf16[1024,512]{1,0:T(8,128)(2,1)S(1)}, u32[]{:S(2)}, u32[]{:S(2)}) collective-permute-start(bf16[1024,512]{1,0:T(8,128)(2,1)S(1)} %copy-done.2), channel_id=1, source_target_pairs={{0,16},{8,24},{16,0},{24,8},{1,17},{9,25},{17,1},{25,9},{2,18},{10... | collective-permute-start | bytes 3145736 | tf_op jit(solution)/shard_map/ppermute | solution.py:423
  75.7 11.3 %collective-permute-start.22 = (bf16[128,1024]{1,0:T(8,128)(2,1)S(1)}, bf16[128,1024]{1,0:T(8,128)(2,1)S(1)}, u32[]{:S(2)}, u32[]{:S(2)}) collective-permute-start(bf16[128,1024]{1,0:T(8,128)(2,1)S(1)} %collective-permute-done.17.refs_0_), channel_id=1, source_target_pairs={{0,4},{1,5},{4,6},{5,7},{6,2},{7,3},{2,0},{3,1},{8,12},{9,13},{12,... | collective-permute-start | bytes 786440 | tf_op jit(solution)/shard_map/ppermute | solution.py:415
  75.7 17.6 %collective-permute-start.28 = (bf16[128,1024]{1,0:T(8,128)(2,1)S(1)}, bf16[128,1024]{1,0:T(8,128)(2,1)S(1)}, u32[]{:S(2)}, u32[]{:S(2)}) collective-permute-start(bf16[128,1024]{1,0:T(8,128)(2,1)S(1)} %collective-permute-done.17.refs_0_), channel_id=1, source_target_pairs={{0,1},{1,0},{4,5},{5,4},{6,7},{7,6},{2,3},{3,2},{8,9},{9,8},{12,13... | collective-permute-start | bytes 786440 | tf_op jit(solution)/shard_map/ppermute | solution.py:418
  83.2 10.2 %collective-permute-start.29 = (bf16[128,1024]{1,0:T(8,128)(2,1)S(1)}, bf16[128,1024]{1,0:T(8,128)(2,1)S(1)}, u32[]{:S(2)}, u32[]{:S(2)}) collective-permute-start(bf16[128,1024]{1,0:T(8,128)(2,1)S(1)} %collective-permute-done.19.refs_1_), channel_id=1, source_target_pairs={{0,1},{1,0},{4,5},{5,4},{6,7},{7,6},{2,3},{3,2},{8,9},{9,8},{12,13... | collective-permute-start | bytes 786440 | tf_op jit(solution)/shard_map/ppermute | solution.py:418
  87.3 13.5 %collective-permute-start.26 = (bf16[128,1024]{1,0:T(8,128)(2,1)S(1)}, bf16[128,1024]{1,0:T(8,128)(2,1)S(1)}, u32[]{:S(2)}, u32[]{:S(2)}) collective-permute-start(bf16[128,1024]{1,0:T(8,128)(2,1)S(1)} %collective-permute-done.24.refs_1_), channel_id=1, source_target_pairs={{0,1},{1,0},{4,5},{5,4},{6,7},{7,6},{2,3},{3,2},{8,9},{9,8},{12,13... | collective-permute-start | bytes 786440 | tf_op jit(solution)/shard_map/ppermute | solution.py:418
  104.7 10.8 %collective-permute-start.40 = (bf16[128,1024]{1,0:T(8,128)(2,1)S(1)}, bf16[128,1024]{1,0:T(8,128)(2,1)S(1)}, u32[]{:S(2)}, u32[]{:S(2)}) collective-permute-start(bf16[128,1024]{1,0:T(8,128)(2,1)S(1)} %get-tuple-element.109), channel_id=1, source_target_pairs={{0,1},{1,0},{4,5},{5,4},{6,7},{7,6},{2,3},{3,2},{8,9},{9,8},{12,13... | collective-permute-start | bytes 786440 | tf_op jit(solution)/shard_map/ppermute | solution.py:512
  106.6 17.0 %collective-permute-start.30 = (bf16[128,1024]{1,0:T(8,128)(2,1)S(1)}, bf16[128,1024]{1,0:T(8,128)(2,1)S(1)}, u32[]{:S(2)}, u32[]{:S(2)}) collective-permute-start(bf16[128,1024]{1,0:T(8,128)(2,1)S(1)} %get-tuple-element.96), channel_id=1, source_target_pairs={{0,1},{1,0},{4,5},{5,4},{6,7},{7,6},{2,3},{3,2},{8,9},{9,8},{12,13... | collective-permute-start | bytes 786440 | tf_op jit(solution)/shard_map/ppermute | solution.py:512
  109.9 13.6 %collective-permute-start.32 = (bf16[128,1024]{1,0:T(8,128)(2,1)S(1)}, bf16[128,1024]{1,0:T(8,128)(2,1)S(1)}, u32[]{:S(2)}, u32[]{:S(2)}) collective-permute-start(bf16[128,1024]{1,0:T(8,128)(2,1)S(1)} %add_convert_fusion.5), channel_id=1, source_target_pairs={{0,4},{1,5},{4,6},{5,7},{6,2},{7,3},{2,0},{3,1},{8,12},{9,13},{12,... | collective-permute-start | bytes 786440 | tf_op jit(solution)/shard_map/ppermute | solution.py:415
  113.9 12.8 %collective-permute-start.39 = (bf16[128,1024]{1,0:T(8,128)(2,1)S(1)}, bf16[128,1024]{1,0:T(8,128)(2,1)S(1)}, u32[]{:S(2)}, u32[]{:S(2)}) collective-permute-start(bf16[128,1024]{1,0:T(8,128)(2,1)S(1)} %get-tuple-element.107), channel_id=1, source_target_pairs={{0,1},{1,0},{4,5},{5,4},{6,7},{7,6},{2,3},{3,2},{8,9},{9,8},{12,13... | collective-permute-start | bytes 786440 | tf_op jit(solution)/shard_map/ppermute | solution.py:512
  115.6 11.2 %collective-permute-start.41 = (bf16[128,1024]{1,0:T(8,128)(2,1)S(1)}, bf16[128,1024]{1,0:T(8,128)(2,1)S(1)}, u32[]{:S(2)}, u32[]{:S(2)}) collective-permute-start(bf16[128,1024]{1,0:T(8,128)(2,1)S(1)} %add_convert_fusion.2), channel_id=1, source_target_pairs={{0,4},{1,5},{4,6},{5,7},{6,2},{7,3},{2,0},{3,1},{8,12},{9,13},{12,... | collective-permute-start | bytes 786440 | tf_op jit(solution)/shard_map/ppermute | solution.py:415
  122.6 11.3 %collective-permute-start.27 = (bf16[128,1024]{1,0:T(8,128)(2,1)S(1)}, bf16[128,1024]{1,0:T(8,128)(2,1)S(1)}, u32[]{:S(2)}, u32[]{:S(2)}) collective-permute-start(bf16[128,1024]{1,0:T(8,128)(2,1)S(1)} %get-tuple-element.92), channel_id=1, source_target_pairs={{0,1},{1,0},{4,5},{5,4},{6,7},{7,6},{2,3},{3,2},{8,9},{9,8},{12,13... | collective-permute-start | bytes 786440 | tf_op jit(solution)/shard_map/ppermute | solution.py:512
  125.2 12.8 %collective-permute-start.38 = (bf16[128,1024]{1,0:T(8,128)(2,1)S(1)}, bf16[128,1024]{1,0:T(8,128)(2,1)S(1)}, u32[]{:S(2)}, u32[]{:S(2)}) collective-permute-start(bf16[128,1024]{1,0:T(8,128)(2,1)S(1)} %get-tuple-element.105), channel_id=1, source_target_pairs={{0,1},{1,0},{4,5},{5,4},{6,7},{7,6},{2,3},{3,2},{8,9},{9,8},{12,13... | collective-permute-start | bytes 786440 | tf_op jit(solution)/shard_map/ppermute | solution.py:512
  126.9 11.1 %collective-permute-start.42 = (bf16[128,1024]{1,0:T(8,128)(2,1)S(1)}, bf16[128,1024]{1,0:T(8,128)(2,1)S(1)}, u32[]{:S(2)}, u32[]{:S(2)}) collective-permute-start(bf16[128,1024]{1,0:T(8,128)(2,1)S(1)} %add_convert_fusion.1), channel_id=1, source_target_pairs={{0,4},{1,5},{4,6},{5,7},{6,2},{7,3},{2,0},{3,1},{8,12},{9,13},{12,... | collective-permute-start | bytes 786440 | tf_op jit(solution)/shard_map/ppermute | solution.py:415
  134.0 10.4 %collective-permute-start.35 = (bf16[128,1024]{1,0:T(8,128)(2,1)S(1)}, bf16[128,1024]{1,0:T(8,128)(2,1)S(1)}, u32[]{:S(2)}, u32[]{:S(2)}) collective-permute-start(bf16[128,1024]{1,0:T(8,128)(2,1)S(1)} %add_convert_fusion.3), channel_id=1, source_target_pairs={{0,4},{1,5},{4,6},{5,7},{6,2},{7,3},{2,0},{3,1},{8,12},{9,13},{12,... | collective-permute-start | bytes 786440 | tf_op jit(solution)/shard_map/ppermute | solution.py:415
  138.1 10.7 %collective-permute-start.43 = (bf16[128,1024]{1,0:T(8,128)(2,1)S(1)}, bf16[128,1024]{1,0:T(8,128)(2,1)S(1)}, u32[]{:S(2)}, u32[]{:S(2)}) collective-permute-start(bf16[128,1024]{1,0:T(8,128)(2,1)S(1)} %get-tuple-element.110), channel_id=1, source_target_pairs={{0,1},{1,0},{4,5},{5,4},{6,7},{7,6},{2,3},{3,2},{8,9},{9,8},{12,13... | collective-permute-start | bytes 786440 | tf_op jit(solution)/shard_map/ppermute | solution.py:512
  (31 other events, 419.8 us)
